TPU v7x, 32 devices: a whole 2x2x4 slice. The times are simulated.
32 devices in a mesh: groups: 2 (over y), dp: 4 (over z), mp: 4 (over x, core).
Axes of the slice: x: 2, y: 2, z: 4, core: 2. Of those that a mesh axis runs over, the one named last changes fastest.
Arguments:
- activations: bfloat16 [1024, 5120], P(('groups', 'dp')), parts along dimension 0, may hold values from -6 to 6
- gradients: bfloat16 [1024, 12800], P(('groups', 'dp')), parts along dimension 0, may hold values from -6 to 6
- input_basis: bfloat16 [5120, 2560], P(None, 'mp'), may hold values from -0.078125 to 0.078125
- output_basis: bfloat16 [12800, 12800], P('dp', 'mp'), may hold values from -0.0546875 to 0.0546875
- lengths: int32 [32], P('groups'), parts along dimension 0, may hold values from 1 to 32, as said below
Outputs:
- corrected_eigenvalues: float32 [5120, 12800], P(('groups', 'dp'), 'mp'), parts along dimension 0
There are 2 independent parts, one for each index of `groups`. A program takes and returns all parts, laid end to end along the dimension named above; an argument that names none is the same for every part. Nothing has to cross between parts.
Inputs may be any that keep to these rules, and one draw needn't show every extreme that they name: `lengths`: at least one sequence has exactly 32 tokens.
All inputs are finite; a program needn't handle non-finite values.
Results may differ from a plain program's by a relative error of at most 0.012.
Values may be sent and summed in bfloat16 or wider, within the bound.
No kernel may reach another device: no remote copies, remote signals or barrier semaphores. Data moves between devices by JAX's collectives and lax.ppermute only.
A program may use at most 320 MiB of HBM per device.

v0:
```python
import jax
import jax.numpy as jnp
from jax import lax
from jax.sharding import PartitionSpec as P


def seq_squares(at_rows, gt_rows, seq_lengths):
    member_count = seq_lengths.shape[0]
    window = at_rows.shape[0] // member_count
    seq_ends = jnp.cumsum(seq_lengths, dtype=jnp.int32)
    starts = seq_ends - seq_lengths
    offsets = jnp.arange(window, dtype=jnp.int32)[:, None]
    totals = jnp.zeros((at_rows.shape[1], gt_rows.shape[1]), jnp.float32)
    for member in range(member_count):
        begin = starts[member]
        at_window = lax.dynamic_slice_in_dim(at_rows, begin, window, 0)
        gt_window = lax.dynamic_slice_in_dim(gt_rows, begin, window, 0)
        inside_rows = offsets < seq_lengths[member]
        masked = jnp.where(inside_rows, at_window, jnp.zeros_like(at_window))
        summed = lax.dot_general(
            masked, gt_window, (((0,), (0,)), ((), ())), preferred_element_type=jnp.float32
        )
        totals = totals + summed * summed
    return totals


def per_device(activations, gradients, input_basis, output_basis, lengths):
    rotated_in = jnp.dot(activations, input_basis, preferred_element_type=jnp.float32).astype(
        jnp.bfloat16
    )
    full_input = lax.all_gather(rotated_in, "mp", axis=1, tiled=True)
    exchanged = lax.all_to_all(gradients, "dp", split_axis=1, concat_axis=0, tiled=True)
    shard_rows = activations.shape[0]
    rotated_out = lax.psum_scatter(
        jnp.dot(exchanged, output_basis, preferred_element_type=jnp.float32).astype(jnp.bfloat16),
        "dp",
        scatter_dimension=0,
        tiled=True,
    )
    shards = lax.axis_size("dp")
    seq_count = lengths.shape[0] // shards
    inverse_count = 1.0 / (shard_rows * shards)
    own_lengths = lax.dynamic_slice_in_dim(lengths, lax.axis_index("dp") * seq_count, seq_count, 0)
    summed = lax.psum_scatter(
        seq_squares(full_input, rotated_out, own_lengths).astype(jnp.bfloat16),
        "dp",
        scatter_dimension=0,
        tiled=True,
    ).astype(jnp.float32)
    return summed * inverse_count


def solution(mesh):
    placed = (
        P(("groups", "dp"), None),
        P(("groups", "dp"), None),
        P(None, "mp"),
        P("dp", "mp"),
        P("groups"),
    )
    return jax.shard_map(
        per_device, mesh=mesh, in_specs=placed, out_specs=P(("groups", "dp"), "mp"), check_vma=False
    )
```

profile of v0, /device:TPU:13, one launch (start us, length us, event | category | flops | bytes accessed | tf_op | source)
XLA Modules:
  0.0 538.9 jit_solution(9835505939070818375)
XLA Ops:
  6.5 0.0 copy-start
  6.5 0.0 reduce-scatter.3.cloned.1.call-start
  6.5 5.7 %copy.6 = bf16[128,12800]{0,1:T(8,128)(2,1)} copy(bf16[128,12800]{1,0:T(8,128)(2,1)} %param.6) | data formatting | bytes 6553600 | tf_op args[1]
  12.2 76.3 %all_to_all.19 = bf16[128,4,3200]{0,2,1:T(8,128)(2,1)} all-to-all(bf16[128,4,3200]{0,2,1:T(8,128)(2,1)} %bitcast.20), channel_id=1, replica_groups=mesh['groups'=2,'dp'=4,'mp'=4] {'dp'}, dimensions={1} | all-to-all | bytes 6553600 | tf_op jit(solution)/shard_map/all_to_all | solution.py:32
  88.5 5.7 %copy.7 = bf16[4,128,3200]{2,1,0:T(8,128)(2,1)} copy(bf16[4,128,3200]{1,2,0:T(8,128)(2,1)} %bitcast.19) | data formatting | bytes 6553600 | tf_op jit(solution)/shard_map/all_to_all | solution.py:32
  94.2 0.0 copy-start.3
  94.2 18.8 %convolution_convert_fusion = bf16[512,3200]{1,0:T(8,128)(2,1)} fusion(bf16[512,3200]{1,0:T(8,128)(2,1)} %bitcast.21, bf16[3200,3200]{1,0:T(8,128)(2,1)} %param.8), kind=kOutput, calls=%fused_computation.2 | convolution fusion | flops 10487398400 | bytes 27033600 | tf_op jit(solution)/shard_map/dot_general | solution.py:35
  113.0 0.0 reduce-scatter.3.cloned.1.call-update
  113.0 0.0 reduce-scatter.5.cloned.1.call-start
  113.0 0.0 copy-done.3
  113.0 0.1 dynamic_slice.27
  113.1 0.1 dynamic-slice_bitcast_fusion
  113.2 0.2 reduce-window.9
  113.4 0.1 bitcast_subtract_fusion
  113.5 0.7 fusion.32
  121.7 0.6 fusion.31
  122.4 0.7 iota_compare_fusion
  123.0 0.6 iota_compare_fusion.1
  123.7 0.6 iota_compare_fusion.2
  124.3 0.6 iota_compare_fusion.3
  124.9 0.0 copy-done
  124.9 4.1 convolution_convert_fusion.1
  129.0 10.1 %all_gather.3 = bf16[128,2560]{1,0:T(8,128)(2,1)S(1)} all-gather(bf16[128,640]{1,0:T(8,128)(2,1)S(1)} %convolution_convert_fusion.1), channel_id=1, replica_groups=mesh['groups'=2,'dp'=4,'mp'=4] {'mp'}, dimensions={1}, use_global_device_ids=true | all-gather | bytes 819200 | tf_op jit(solution)/shard_map/all_gather | solution.py:31
  139.1 37.9 %reduce-scatter.3.cloned.1.call-done = bf16[128,3200]{1,0:T(8,128)(2,1)} async-done(((bf16[512,3200]{1,0:T(8,128)(2,1)}), bf16[128,3200]{1,0:T(8,128)(2,1)}) %reduce-scatter.3.cloned.1.call-update) | async-done | bytes 819216 | tf_op jit(solution)/shard_map/reduce_scatter | solution.py:34
  176.9 0.0 copy-start.2
  176.9 14.0 %fusion.1 = f32[2560,3200]{1,0:T(8,128)} fusion(bf16[128,3200]{1,0:T(8,128)(2,1)} %reduce-scatter.3.cloned.1.call-done, s32[]{:T(128)S(6)} %select_n.37, bf16[128,2560]{1,0:T(8,128)(2,1)S(1)} %all_gather.3, pred[32]{0:T(512)(128)(4,1)S(1)} %iota_compare_fusion.1), kind=kOutput, calls=%fused_computation.5 | convolution fusion | flops 524369920 | bytes 33138176 | tf_op jit(solution)/shard_map/dot_general | solution.py:20
  190.9 0.0 copy-done.2
  191.0 13.0 %fusion.3 = f32[2560,3200]{1,0:T(8,128)} fusion(bf16[128,3200]{1,0:T(8,128)(2,1)S(1)} %copy-done.2, s32[]{:T(128)S(6)} %select_n.35, bf16[128,2560]{1,0:T(8,128)(2,1)S(1)} %all_gather.3, pred[32]{0:T(512)(128)(4,1)S(1)} %iota_compare_fusion.2), kind=kOutput, calls=%fused_computation.7 | convolution fusion | flops 524369920 | bytes 33138176 | tf_op jit(solution)/shard_map/dot_general | solution.py:20
  203.9 13.1 %fusion.5 = f32[2560,3200]{1,0:T(8,128)} fusion(bf16[128,3200]{1,0:T(8,128)(2,1)S(1)} %copy-done.2, s32[]{:T(128)S(6)} %select_n.33, bf16[128,2560]{1,0:T(8,128)(2,1)S(1)} %all_gather.3, pred[32]{0:T(512)(128)(4,1)S(1)} %iota_compare_fusion.3), kind=kOutput, calls=%fused_computation.9 | convolution fusion | flops 524369920 | bytes 33138176 | tf_op jit(solution)/shard_map/dot_general | solution.py:20
  217.0 37.3 %add_convert_fusion = bf16[2560,3200]{1,0:T(8,128)(2,1)} fusion(f32[2560,3200]{1,0:T(8,128)} %fusion.1, f32[2560,3200]{1,0:T(8,128)} %fusion.3, f32[2560,3200]{1,0:T(8,128)} %fusion.5, bf16[128,3200]{1,0:T(8,128)(2,1)S(1)} %copy-done.2, s32[]{:T(128)S(6)} %select_n.39, bf16[128,2560]{1,0:T(8,128)(2,1)S(1)} %all_gather.3, pred[32]{0:T(512)(128)(4,1)S(1)} %iota_compare_fusion), kind=kOutput, calls=%fused_computation | convolution fusion | flops 589905920 | bytes 115058176 | tf_op jit(solution)/shard_map/dot_general | solution.py:20
  254.4 0.0 reduce-scatter.5.cloned.1.call-update
  254.4 0.0 copy-start.1
  254.4 271.6 %reduce-scatter.5.cloned.1.call-done = bf16[640,3200]{1,0:T(8,128)(2,1)} async-done(((bf16[2560,3200]{1,0:T(8,128)(2,1)}), bf16[640,3200]{1,0:T(8,128)(2,1)}) %reduce-scatter.5.cloned.1.call-update) | async-done | bytes 4096016 | tf_op jit(solution)/shard_map/reduce_scatter | solution.py:44
  526.0 6.0 %convert_multiply_fusion = f32[640,3200]{1,0:T(8,128)} fusion(bf16[640,3200]{1,0:T(8,128)(2,1)} %reduce-scatter.5.cloned.1.call-done), kind=kLoop, calls=%fused_computation.1 | loop fusion | flops 4096000 | bytes 12288000 | tf_op jit(solution)/shard_map/mul | solution.py:50
  532.1 0.0 copy-done.1
Async XLA Ops:
  6.5 118.4 %copy-start = (bf16[128,5120]{1,0:T(8,128)(2,1)S(1)}, bf16[128,5120]{1,0:T(8,128)(2,1)}, u32[]{:S(2)}) copy-start(bf16[128,5120]{1,0:T(8,128)(2,1)} %param.5) | copy-start | bytes 3932164
  6.5 170.4 %reduce-scatter.3.cloned.1.call-start = ((), (), s32[]{:S(2)}) async-start(), calls=%async_computation.3 | async-start | bytes 4096000 | tf_op jit(solution)/shard_map/reduce_scatter | solution.py:34
  94.2 18.9 %copy-start.3 = (s32[16]{0:T(128)S(1)}, s32[16]{0:T(128)}, u32[]{:S(2)}) copy-start(s32[16]{0:T(128)} %param.9) | copy-start | bytes 196
  113.0 413.1 %reduce-scatter.5.cloned.1.call-start = ((), (), s32[]{:S(2)}) async-start(), calls=%async_computation.4 | async-start | bytes 20480000 | tf_op jit(solution)/shard_map/reduce_scatter | solution.py:44
  176.9 14.0 %copy-start.2 = (bf16[128,3200]{1,0:T(8,128)(2,1)S(1)}, bf16[128,3200]{1,0:T(8,128)(2,1)}, u32[]{:S(2)}) copy-start(bf16[128,3200]{1,0:T(8,128)(2,1)} %reduce-scatter.3.cloned.1.call-done) | copy-start | bytes 2457604
  254.4 277.7 %copy-start.1 = (bf16[128,5120]{1,0:T(8,128)(2,1)S(1)}, bf16[128,5120]{1,0:T(8,128)(2,1)}, u32[]{:S(2)}) copy-start(bf16[128,5120]{1,0:T(8,128)(2,1)} %param.5) | copy-start | bytes 3932164
Sparse Core Ops, SparseCore 0:
  113.1 63.7 reduce-scatter.2
  254.5 271.4 reduce-scatter.4
where the time goes:
time: 544 us; the launch traced here: 539 us
  waiting for transfers between devices  310 us (57%)
  matrix products  100 us (18%)
  blocking collectives  86.4 us (16%)
  between operations  21.1 us (4%)
  local copies, waits for them, and re-layouts  12.8 us (2%)
  other arithmetic  8.82 us (2%)
    reduce_scatter x1, waiting for transfers between devices, per_device(): lax.psum_scatter(seq_squares(full_input, rotated_out, own_lengths).astype...  272 us
    dot_general x4, matrix products, seq_squares(): lax.dot_general(masked, gt_window, (((0,), (0,)), ((), ())), preferred_el...  77.4 us
    all_to_all x1, blocking collectives, per_device(): lax.all_to_all(gradients, 'dp', split_axis=1, concat_axis=0, tiled=True)  76.3 us
    reduce_scatter x1, waiting for transfers between devices, per_device(): lax.psum_scatter(jnp.dot(exchanged, output_basis, preferred_element_type=...  37.9 us
    dot_general x1, matrix products, per_device(): jnp.dot(exchanged, output_basis, preferred_element_type=jnp.float32)  18.8 us
  transfers between devices with their start and end apart: 2, of which 2 were waited for; matrix products, arithmetic and copies ran while one was open for 2% of the time, Pallas kernels for 0%

commit v1 on v0

v1 whole, which is shorter than its diff:
```python
import functools

import jax
import jax.numpy as jnp
from jax import lax
from jax.experimental import pallas as pl
from jax.experimental.pallas import tpu as pltpu
from jax.sharding import PartitionSpec as P

TILE = 256
WINDOW = 128
ALIGN = 16
VMEM_LIMIT = 48 * 1024 * 1024


def column_chunks(width):
    tiles = -(-width // TILE)
    count = min(5, tiles)
    edges = [tiles * c // count for c in range(count + 1)]
    return [
        (lo * TILE, min(hi * TILE, width) - lo * TILE) for lo, hi in zip(edges[:-1], edges[1:])
    ]


def compact_kernel(tgt, lim, pieces, *refs):
    sources, out, buf, sems = refs[: len(pieces)], refs[-3], refs[-2], refs[-1]
    copies = []
    row = 0
    for j, size in enumerate(pieces):
        copies.append(pltpu.make_async_copy(sources[j], buf.at[pl.ds(row, size)], sems.at[j]))
        copies[-1].start()
        row += size
    selectors = []
    for j, size in enumerate(pieces):
        place = lax.broadcasted_iota(jnp.int32, (out.shape[0], size), 0)
        token = lax.broadcasted_iota(jnp.int32, (out.shape[0], size), 1) + tgt[j]
        selectors.append(jnp.where((place == token) & (place < lim[j]), 1.0, 0.0))
    selector = jnp.concatenate(selectors, axis=1).astype(jnp.bfloat16)
    for copy in copies:
        copy.wait()
    width = out.shape[1]
    step = 640 if width % 640 == 0 else width
    for lo in range(0, width, step):
        out[:, lo : lo + step] = jnp.dot(
            selector, buf[:, lo : lo + step], preferred_element_type=jnp.float32
        ).astype(out.dtype)


def compact(pieces, targets, limits, rows):
    sizes = tuple(p.shape[0] for p in pieces)
    width = pieces[0].shape[1]

    def kernel(tgt, lim, *refs):
        compact_kernel(tgt, lim, sizes, *refs)

    return pl.pallas_call(
        kernel,
        grid_spec=pltpu.PrefetchScalarGridSpec(
            num_scalar_prefetch=2,
            grid=(),
            in_specs=[pl.BlockSpec(memory_space=pl.ANY)] * len(pieces),
            out_specs=pl.BlockSpec(memory_space=pltpu.VMEM),
            scratch_shapes=[
                pltpu.VMEM((sum(sizes), width), jnp.bfloat16),
                pltpu.SemaphoreType.DMA((len(pieces),)),
            ],
        ),
        out_shape=jax.ShapeDtypeStruct((rows, width), jnp.bfloat16),
        compiler_params=pltpu.CompilerParams(vmem_limit_bytes=VMEM_LIMIT),
        name="compact_rows",
    )(targets, limits, *pieces)


def rotate_kernel(rows_ref, basis_ref, out_ref):
    out_ref[...] = jnp.dot(
        rows_ref[...], basis_ref[...], preferred_element_type=jnp.float32
    ).astype(out_ref.dtype)


def rotate(rows, basis, first, size):
    depth = basis.shape[0]
    begin = first // TILE
    return pl.pallas_call(
        rotate_kernel,
        grid=(-(-size // TILE),),
        in_specs=[
            pl.BlockSpec(rows.shape, lambda j: (0, 0)),
            pl.BlockSpec((depth, TILE), lambda j: (0, begin + j)),
        ],
        out_specs=pl.BlockSpec((rows.shape[0], TILE), lambda j: (0, j)),
        out_shape=jax.ShapeDtypeStruct((rows.shape[0], size), jnp.bfloat16),
        compiler_params=pltpu.CompilerParams(vmem_limit_bytes=VMEM_LIMIT),
        cost_estimate=pl.CostEstimate(
            flops=2 * rows.shape[0] * depth * size,
            bytes_accessed=2 * depth * size + 2 * rows.size,
            transcendentals=0,
        ),
        name="rotate_chunk",
    )(rows, basis)


def squares_kernel(seqs, scale, window_starts, at_ref, gt_ref, *refs):
    out_ref = refs[-1]
    for n in range(seqs):
        start = pl.multiple_of(window_starts[n], ALIGN)
        summed = jnp.dot(
            at_ref[:, n * WINDOW : (n + 1) * WINDOW],
            gt_ref[pl.ds(start, WINDOW), :],
            preferred_element_type=jnp.float32,
        )
        squared = summed * summed
        if n == 0:
            out_ref[...] = squared
        elif n < seqs - 1:
            out_ref[...] += squared
        else:
            out_ref[...] = (out_ref[...] + squared) * scale


def squares(window_starts, at_windows, gt_chunk, scale, first, total_width, previous):
    seqs = window_starts.shape[0]
    directions = at_windows.shape[0]
    rows, size = gt_chunk.shape
    begin = first // TILE
    in_specs = [
        pl.BlockSpec(at_windows.shape, lambda j, ws: (0, 0)),
        pl.BlockSpec((rows, TILE), lambda j, ws: (0, j)),
    ]
    operands = [window_starts, at_windows, gt_chunk]
    aliases = {}
    if previous is not None:
        in_specs.append(pl.BlockSpec(memory_space=pl.ANY))
        operands.append(previous)
        aliases = {3: 0}
    return pl.pallas_call(
        functools.partial(squares_kernel, seqs, scale),
        grid_spec=pltpu.PrefetchScalarGridSpec(
            num_scalar_prefetch=1,
            grid=(-(-size // TILE),),
            in_specs=in_specs,
            out_specs=pl.BlockSpec((directions, TILE), lambda j, ws: (0, begin + j)),
        ),
        out_shape=jax.ShapeDtypeStruct((directions, total_width), jnp.float32),
        input_output_aliases=aliases,
        compiler_params=pltpu.CompilerParams(vmem_limit_bytes=VMEM_LIMIT),
        cost_estimate=pl.CostEstimate(
            flops=2 * seqs * directions * size * WINDOW,
            bytes_accessed=4 * directions * size + 2 * rows * size,
            transcendentals=0,
        ),
        name="sum_squares",
    )(*operands)


def add_rounded(a, b):
    return (a.astype(jnp.float32) + b.astype(jnp.float32)).astype(jnp.bfloat16)


def exchange_gradients(gradients, shards, parts):
    d, m = lax.axis_index("dp"), lax.axis_index("mp")
    rows, hidden = gradients.shape
    width = hidden // shards
    if shards == 4 and parts == 4:
        share = rows // parts
        mine = lax.dynamic_slice_in_dim(gradients, m * share, share, 0)
        own = lax.dynamic_slice_in_dim(gradients, d * width, width, 1)
        pieces = [(own, d, 0)]
        far = []
        for k in (2, 1, 3):
            block = lax.dynamic_slice_in_dim(mine, lax.rem(d + k, shards) * width, width, 1)
            received = lax.ppermute(block, "dp", [(e, (e + k) % shards) for e in range(shards)])
            far.append((received, lax.rem(d + shards - k, shards)))
        for received, e in far:
            crossed = lax.ppermute(received, "mp", [(p, p ^ 2) for p in range(parts)])
            pieces.append((received, e, m * share))
            pieces.append((crossed, e, (m ^ 2) * share))
            for piece, part in ((received, m ^ 1), (crossed, m ^ 3)):
                swapped = lax.ppermute(piece, "mp", [(p, p ^ 1) for p in range(parts)])
                pieces.append((swapped, e, part * share))
        return pieces
    exchanged = lax.all_to_all(gradients, "dp", split_axis=1, concat_axis=0, tiled=True)
    return [(exchanged[e * rows : (e + 1) * rows], e, 0) for e in range(shards)]


def exchange_inputs(rotated_in, shards, parts):
    d, m = lax.axis_index("dp"), lax.axis_index("mp")
    if shards == 4 and parts == 4:
        at = lambda e, p: e * parts + p
        gathered = [rotated_in]
        for k in range(1, shards):
            pairs = [(at((p + k) % shards, p), at(p, p)) for p in range(parts)]
            gathered.append(lax.ppermute(rotated_in, ("dp", "mp"), pairs))
        held = jnp.concatenate(gathered, axis=0)
        crossed = lax.ppermute(held, ("dp", "mp"), [(at(p, p), at(p, p ^ 2)) for p in range(parts)])
        held = jnp.where(m == d, held, crossed)
        swapped = lax.ppermute(
            held,
            ("dp", "mp"),
            [(at(p, p), at(p, p ^ 1)) for p in range(parts)]
            + [(at(p, p ^ 2), at(p, p ^ 3)) for p in range(parts)],
        )
        held = jnp.where((m == d) | (m == (d ^ 2)), held, swapped)
        return held, lax.rem(d + jnp.arange(shards, dtype=jnp.int32), shards)
    full = lax.all_gather(rotated_in, "mp", axis=1, tiled=True)
    held = lax.all_to_all(full, "dp", split_axis=1, concat_axis=0, tiled=True)
    return held, jnp.arange(shards, dtype=jnp.int32)


def sum_over_shards(parts, shards):
    if shards != 4:
        return [lax.psum(part, "dp") for part in parts]
    d = lax.axis_index("dp")
    middle = (d == 1) | (d == 2)
    sums = []
    for part in parts:
        pair = add_rounded(part, lax.ppermute(part, "dp", [(0, 1), (3, 2)]))
        both = add_rounded(pair, lax.ppermute(pair, "dp", [(1, 2), (2, 1)]))
        sums.append(jnp.where(middle, both, lax.ppermute(both, "dp", [(1, 0), (2, 3)])))
    return sums


def per_device(activations, gradients, input_basis, output_basis, lengths):
    shards, parts = lax.axis_size("dp"), lax.axis_size("mp")
    shard_rows = activations.shape[0]
    rows = shard_rows * shards
    seqs = lengths.shape[0]
    per_shard = seqs // shards

    seq_ends = jnp.cumsum(lengths, dtype=jnp.int32)
    seq_starts = seq_ends - lengths
    shard_ends = seq_ends[per_shard - 1 :: per_shard]
    shard_starts = seq_starts[::per_shard]
    window_starts = jnp.minimum(seq_starts // ALIGN * ALIGN, rows - WINDOW)

    pieces = exchange_gradients(gradients, shards, parts)
    rotated_in = jnp.dot(activations, input_basis, preferred_element_type=jnp.float32).astype(
        jnp.bfloat16
    )
    held, order = exchange_inputs(rotated_in, shards, parts)

    piece_shards = jnp.stack([jnp.asarray(e, jnp.int32) for _, e, _ in pieces])
    piece_rows = jnp.stack([jnp.asarray(r, jnp.int32) for _, _, r in pieces])
    targets = shard_starts[piece_shards] + piece_rows
    limits = shard_ends[piece_shards]
    compacted = compact([p for p, _, _ in pieces], targets, limits, rows)

    place = window_starts[:, None] + jnp.arange(WINDOW, dtype=jnp.int32)[None, :]
    inside = (place >= seq_starts[:, None]) & (place < seq_ends[:, None])
    seq_shard = jnp.arange(seqs, dtype=jnp.int32)[:, None] // per_shard
    token = place - jnp.repeat(shard_starts, per_shard)[:, None] + seq_shard * shard_rows
    token = jnp.where(inside, token, -1).reshape(-1)
    held_token = (
        order[:, None] * shard_rows + jnp.arange(shard_rows, dtype=jnp.int32)[None, :]
    ).reshape(-1)
    selector = (held_token[:, None] == token[None, :]).astype(jnp.bfloat16)
    at_windows = lax.dot_general(
        held, selector, (((0,), (0,)), ((), ())), preferred_element_type=jnp.float32
    ).astype(jnp.bfloat16)

    width = output_basis.shape[1]
    chunks = column_chunks(width)
    partials = [rotate(compacted, output_basis, first, size) for first, size in chunks]
    result = None
    for (first, _), gt_chunk in zip(chunks, sum_over_shards(partials, shards)):
        result = squares(window_starts, at_windows, gt_chunk, 1.0 / rows, first, width, result)
    return result


def solution(mesh):
    placed = (
        P(("groups", "dp"), None),
        P(("groups", "dp"), None),
        P(None, "mp"),
        P("dp", "mp"),
        P("groups"),
    )
    return jax.shard_map(
        per_device, mesh=mesh, in_specs=placed, out_specs=P(("groups", "dp"), "mp"), check_vma=False
    )
```

time: 544 us -> 252 us (0.46)
  waiting for transfers between devices: 310 us -> 115 us
  matrix products: 100 us -> 5.83 us
  blocking collectives: 86.4 us -> 0 us
  Pallas kernels: 0 us -> 58.1 us
  starting transfers between devices: 0.04 us -> 56.8 us
  between operations: 21.1 us -> 0.56 us
    reduce_scatter x2 -> x0, waiting for transfers between devices: 310 us -> none  [the longest x1 272 us: per_device(): lax.psum_scatter(seq_squares(full_input, rotated_out, own_lengths).astype...]
    ppermute x0 -> x32, waiting for transfers between devices: none -> 115 us  [the longest x5 44.9 us: sum_over_shards(): pair = add_rounded(part, lax.ppermute(part, 'dp', [(0, 1), (3, 2)]))]
    dot_general x5 -> x1, matrix products: 96.2 us -> 1.77 us  [per_device(): lax.dot_general(held, selector, (((0,), (0,)), ((), ())), preferred_eleme...]
    all_to_all x1 -> x0, blocking collectives: 76.3 us -> none  [per_device(): lax.all_to_all(gradients, 'dp', split_axis=1, concat_axis=0, tiled=True)]
    pallas_call x0 -> x11, Pallas kernels: none -> 58.1 us  [the longest x5 27.4 us: squares(): pl.pallas_call(functools.partial(squares_kernel, seqs, scale), grid_spec=...]
    ppermute x0 -> x32, starting transfers between devices: none -> 56.8 us  [the longest x6 15.8 us: exchange_gradients(): swapped = lax.ppermute(piece, 'mp', [(p, p ^ 1) for p in range(parts)])]
    all_gather x1 -> x0, blocking collectives: 10.1 us -> none  [per_device(): full_input = lax.all_gather(rotated_in, 'mp', axis=1, tiled=True)]
    mul x1 -> x2, other arithmetic: 6.02 us -> 0.01 us  [the longest x1 0.01 us: per_device(): order[:, None] * shard_rows]
  transfers between devices with their start and end apart: 2 -> 32, of which waited for: 2 -> 13; matrix products, arithmetic and copies ran while one was open for 2% -> 4% of each run, Pallas kernels for 0% -> 18%
where the time goes in v1:
time: 252 us; the launch traced here: 249 us
  waiting for transfers between devices  115 us (46%)
  Pallas kernels  58.1 us (23%)
  starting transfers between devices  56.8 us (23%)
  local copies, waits for them, and re-layouts  7.89 us (3%)
  matrix products  5.83 us (2%)
  other arithmetic  4.57 us (2%)
    ppermute x5, waiting for transfers between devices, sum_over_shards(): pair = add_rounded(part, lax.ppermute(part, 'dp', [(0, 1), (3, 2)]))  44.9 us
    ppermute x5, waiting for transfers between devices, sum_over_shards(): lax.ppermute(both, 'dp', [(1, 0), (2, 3)])  34.7 us
    pallas_call x5, Pallas kernels, squares(): pl.pallas_call(functools.partial(squares_kernel, seqs, scale), grid_spec=...  27.4 us
    ppermute x5, waiting for transfers between devices, sum_over_shards(): both = add_rounded(pair, lax.ppermute(pair, 'dp', [(1, 2), (2, 1)]))  24.9 us
    pallas_call x5, Pallas kernels, rotate(): pl.pallas_call(rotate_kernel, grid=(-(-size // TILE),), in_specs=[pl.Bloc...  22 us
    ppermute x6, starting transfers between devices, exchange_gradients(): swapped = lax.ppermute(piece, 'mp', [(p, p ^ 1) for p in range(parts)])  15.8 us
    ppermute x5, starting transfers between devices, sum_over_shards(): both = add_rounded(pair, lax.ppermute(pair, 'dp', [(1, 2), (2, 1)]))  11.2 us
    pallas_call x1, Pallas kernels, compact(): pl.pallas_call(kernel, grid_spec=pltpu.PrefetchScalarGridSpec(num_scalar_...  8.74 us
  transfers between devices with their start and end apart: 32, of which 13 were waited for; matrix products, arithmetic and copies ran while one was open for 4% of the time, Pallas kernels for 18%

profile of v1, /device:TPU:13, one launch (start us, length us, event | category | flops | bytes accessed | tf_op | source)
XLA Modules:
  0.0 248.8 jit_solution(17756159921491673136)
XLA Ops:
  0.0 1.3 copy-done
  1.3 4.1 %convolution_convert_fusion = bf16[128,640]{1,0:T(8,128)(2,1)S(1)} fusion(bf16[128,5120]{1,0:T(8,128)(2,1)S(1)} %copy-done, bf16[5120,640]{1,0:T(8,128)(2,1)} %param.7), kind=kOutput, calls=%fused_computation.13 | convolution fusion | flops 838942720 | bytes 8028160 | tf_op jit(solution)/shard_map/dot_general | solution.py:236
  5.4 1.3 collective-permute-start.2
  6.7 1.3 collective-permute-start.1
  8.0 1.5 fusion.16
  9.5 2.1 collective-permute-start.13
  11.6 1.5 collective-permute-start.5
  13.2 2.3 collective-permute-start.9
  18.9 1.4 collective-permute-done.13.refs_9_
  20.3 12.2 %collective-permute-start.15 = (bf16[32,3200]{1,0:T(8,128)(2,1)S(1)}, bf16[32,3200]{1,0:T(8,128)(2,1)S(1)}, u32[]{:S(2)}, u32[]{:S(2)}) collective-permute-start(bf16[32,3200]{1,0:T(8,128)(2,1)S(1)} %collective-permute-done.13.refs_9_), channel_id=1, source_target_pairs={{0,1},{1,0},{2,3},{3,2},{4,5},{5,4},{6,7},{7,6},{8,9},{9,8},{10,11... | collective-permute-start | bytes 614408 | tf_op jit(solution)/shard_map/ppermute | solution.py:178
  32.5 1.5 collective-permute-start.6
  34.0 2.1 collective-permute-start.10
  37.0 2.2 collective-permute-done.14.refs_10_
  40.4 3.3 %collective-permute-done.6.refs_2_ = bf16[32,3200]{1,0:T(8,128)(2,1)S(1)} collective-permute-done((bf16[32,3200]{1,0:T(8,128)(2,1)S(1)}, bf16[32,3200]{1,0:T(8,128)(2,1)S(1)}, u32[]{:S(2)}, u32[]{:S(2)}) %collective-permute-start.6) | collective-permute-done | bytes 204832 | tf_op jit(solution)/shard_map/ppermute | solution.py:174
  44.7 3.3 %collective-permute-done.10.refs_6_ = bf16[32,3200]{1,0:T(8,128)(2,1)S(1)} collective-permute-done((bf16[32,3200]{1,0:T(8,128)(2,1)S(1)}, bf16[32,3200]{1,0:T(8,128)(2,1)S(1)}, u32[]{:S(2)}, u32[]{:S(2)}) %collective-permute-start.10) | collective-permute-done | bytes 204832 | tf_op jit(solution)/shard_map/ppermute | solution.py:174
  51.4 1.9 collective-permute-start.3
  53.3 8.7 %compact_rows.1.rows_ref = bf16[512,3200]{1,0:T(8,128)(2,1)} custom-call(s32[13]{0:T(128)S(1)} %add.160.tgt, s32[13]{0:T(128)S(1)} %gather_fusion.1, bf16[128,3200]{1,0:T(8,128)(2,1)S(1)} %constant_dynamic-slice_fusion.refs_0_, bf16[32,3200]{1,0:T(8,128)(2,1)S(1)} %collective-permute-done.5.refs_1_, bf16[32,3200]{1,0:T(8,128)(2,1)S(1)} %collective-permute-done.6.refs_2_, ...), custom_call_target="tpu_custom_call" | custom-call | tf_op jit(solution)/shard_map/compact_rows/pallas_call | solution.py:56
  62.1 1.9 copy-done.2
  64.0 5.0 %rotate_chunk.8 = bf16[512,768]{1,0:T(8,128)(2,1)S(1)} custom-call(bf16[512,3200]{1,0:T(8,128)(2,1)S(1)} %copy-done.2, bf16[3200,3200]{1,0:T(8,128)(2,1)} %basis_ref.9), custom_call_target="tpu_custom_call" | custom-call | flops 2516582400 | bytes 8192000 | tf_op jit(solution)/shard_map/rotate_chunk/pallas_call | solution.py:83
  69.0 3.6 %rotate_chunk.7 = bf16[512,512]{1,0:T(8,128)(2,1)S(1)} custom-call(bf16[512,3200]{1,0:T(8,128)(2,1)S(1)} %copy-done.2, bf16[3200,3200]{1,0:T(8,128)(2,1)} %basis_ref.9), custom_call_target="tpu_custom_call" | custom-call | flops 1677721600 | bytes 6553600 | tf_op jit(solution)/shard_map/rotate_chunk/pallas_call | solution.py:83
  73.9 5.0 %rotate_chunk.6 = bf16[512,768]{1,0:T(8,128)(2,1)S(1)} custom-call(bf16[512,3200]{1,0:T(8,128)(2,1)S(1)} %copy-done.2, bf16[3200,3200]{1,0:T(8,128)(2,1)} %basis_ref.9), custom_call_target="tpu_custom_call" | custom-call | flops 2516582400 | bytes 8192000 | tf_op jit(solution)/shard_map/rotate_chunk/pallas_call | solution.py:83
  78.9 3.6 %rotate_chunk.9 = bf16[512,512]{1,0:T(8,128)(2,1)S(1)} custom-call(bf16[512,3200]{1,0:T(8,128)(2,1)S(1)} %copy-done.2, bf16[3200,3200]{1,0:T(8,128)(2,1)} %basis_ref.9), custom_call_target="tpu_custom_call" | custom-call | flops 1677721600 | bytes 6553600 | tf_op jit(solution)/shard_map/rotate_chunk/pallas_call | solution.py:83
  82.5 1.4 collective-permute-start.29
  84.0 4.8 %rotate_chunk.5 = bf16[512,640]{1,0:T(8,128)(2,1)S(1)} custom-call(bf16[512,3200]{1,0:T(8,128)(2,1)S(1)} %copy-done.2, bf16[3200,3200]{1,0:T(8,128)(2,1)} %basis_ref.9), custom_call_target="tpu_custom_call" | custom-call | flops 2097152000 | bytes 7372800 | tf_op jit(solution)/shard_map/rotate_chunk/pallas_call | solution.py:83
  93.9 1.3 collective-permute-start.4
  95.3 4.3 %collective-permute-done.29 = bf16[512,512]{1,0:T(8,128)(2,1)S(1)} collective-permute-done((bf16[512,512]{1,0:T(8,128)(2,1)S(1)}, bf16[512,512]{1,0:T(8,128)(2,1)S(1)}, u32[]{:S(2)}, u32[]{:S(2)}) %collective-permute-start.29) | collective-permute-done | bytes 524320 | tf_op jit(solution)/shard_map/ppermute | solution.py:216
  99.7 1.9 collective-permute-start.24
  101.7 12.0 %collective-permute-done.17 = bf16[512,640]{1,0:T(8,128)(2,1)S(1)} collective-permute-done((bf16[512,640]{1,0:T(8,128)(2,1)S(1)}, bf16[512,640]{1,0:T(8,128)(2,1)S(1)}, u32[]{:S(2)}, u32[]{:S(2)}) %collective-permute-start.17) | collective-permute-done | bytes 655392 | tf_op jit(solution)/shard_map/ppermute | solution.py:216
  113.7 1.9 collective-permute-start.30
  115.8 14.8 %collective-permute-done.20 = bf16[512,768]{1,0:T(8,128)(2,1)S(1)} collective-permute-done((bf16[512,768]{1,0:T(8,128)(2,1)S(1)}, bf16[512,768]{1,0:T(8,128)(2,1)S(1)}, u32[]{:S(2)}, u32[]{:S(2)}) %collective-permute-start.20) | collective-permute-done | bytes 786464 | tf_op jit(solution)/shard_map/ppermute | solution.py:216
  130.5 2.1 collective-permute-start.18
  132.8 13.8 %collective-permute-done.26 = bf16[512,768]{1,0:T(8,128)(2,1)S(1)} collective-permute-done((bf16[512,768]{1,0:T(8,128)(2,1)S(1)}, bf16[512,768]{1,0:T(8,128)(2,1)S(1)}, u32[]{:S(2)}, u32[]{:S(2)}) %collective-permute-start.26) | collective-permute-done | bytes 786464 | tf_op jit(solution)/shard_map/ppermute | solution.py:216
  146.7 1.9 collective-permute-start.21
  148.8 3.4 %collective-permute-start.27 = (bf16[512,768]{1,0:T(8,128)(2,1)S(1)}, bf16[512,768]{1,0:T(8,128)(2,1)S(1)}, u32[]{:S(2)}, u32[]{:S(2)}) collective-permute-start(bf16[512,768]{1,0:T(8,128)(2,1)S(1)} %add_convert_fusion.1), channel_id=1, source_target_pairs={{4,8},{8,4},{5,9},{9,5},{6,10},{10,6},{7,11},{11,7},{20,24},{24,20... | collective-permute-start | bytes 2359304 | tf_op jit(solution)/shard_map/ppermute | solution.py:217
  152.2 1.8 fusion.2.at_ref
  154.1 1.3 collective-permute-start.25
  155.6 1.3 collective-permute-start.31
  157.1 1.3 collective-permute-start.19
  158.4 9.6 %collective-permute-done.21 = bf16[512,768]{1,0:T(8,128)(2,1)S(1)} collective-permute-done((bf16[512,768]{1,0:T(8,128)(2,1)S(1)}, bf16[512,768]{1,0:T(8,128)(2,1)S(1)}, u32[]{:S(2)}, u32[]{:S(2)}) %collective-permute-start.21) | collective-permute-done | bytes 786464 | tf_op jit(solution)/shard_map/ppermute | solution.py:217
  168.2 1.3 collective-permute-start.22
  169.5 15.3 %collective-permute-done.27 = bf16[512,768]{1,0:T(8,128)(2,1)S(1)} collective-permute-done((bf16[512,768]{1,0:T(8,128)(2,1)S(1)}, bf16[512,768]{1,0:T(8,128)(2,1)S(1)}, u32[]{:S(2)}, u32[]{:S(2)}) %collective-permute-start.27) | collective-permute-done | bytes 786464 | tf_op jit(solution)/shard_map/ppermute | solution.py:217
  185.0 1.3 collective-permute-start.28
  186.5 4.5 %sum_squares.5.refs_0_ = f32[640,3200]{1,0:T(8,128)} custom-call(s32[16]{0:T(128)S(1)} %get-tuple-element.5.window_starts, bf16[640,2048]{1,0:T(8,128)(2,1)S(1)} %fusion.2.at_ref, bf16[512,512]{1,0:T(8,128)(2,1)S(1)} %broadcast_select_fusion.4.gt_ref), custom_call_target="tpu_custom_call" | custom-call | flops 1342177280 | bytes 1835008 | tf_op jit(solution)/shard_map/sum_squares/pallas_call | solution.py:135
  192.2 33.6 %collective-permute-done.28 = bf16[512,768]{1,0:T(8,128)(2,1)S(1)} collective-permute-done((bf16[512,768]{1,0:T(8,128)(2,1)S(1)}, bf16[512,768]{1,0:T(8,128)(2,1)S(1)}, u32[]{:S(2)}, u32[]{:S(2)}) %collective-permute-start.28) | collective-permute-done | bytes 786464 | tf_op jit(solution)/shard_map/ppermute | solution.py:218
  225.9 6.1 %sum_squares.6.refs_0_ = f32[640,3200]{1,0:T(8,128)} custom-call(s32[16]{0:T(128)S(1)} %get-tuple-element.5.window_starts, bf16[640,2048]{1,0:T(8,128)(2,1)S(1)} %fusion.2.at_ref, bf16[512,768]{1,0:T(8,128)(2,1)S(1)} %broadcast_select_fusion.gt_ref, f32[640,3200]{1,0:T(8,128)} %sum_squares.5.refs_0_), custom_call_target="tpu_custom_call", output_to_operand_aliasing={{}: (3, {})} | custom-call | flops 2013265920 | bytes 2752512 | tf_op jit(solution)/shard_map/sum_squares/pallas_call | solution.py:135
  232.0 4.5 %sum_squares.7.refs_0_ = f32[640,3200]{1,0:T(8,128)} custom-call(s32[16]{0:T(128)S(1)} %get-tuple-element.5.window_starts, bf16[640,2048]{1,0:T(8,128)(2,1)S(1)} %fusion.2.at_ref, bf16[512,512]{1,0:T(8,128)(2,1)S(1)} %broadcast_select_fusion.5.gt_ref, f32[640,3200]{1,0:T(8,128)} %sum_squares.6.refs_0_), custom_call_target="tpu_custom_call", output_to_operand_aliasing={{}: (3, {})} | custom-call | flops 1342177280 | bytes 1835008 | tf_op jit(solution)/shard_map/sum_squares/pallas_call | solution.py:135
  236.6 6.1 %sum_squares.8.refs_0_ = f32[640,3200]{1,0:T(8,128)} custom-call(s32[16]{0:T(128)S(1)} %get-tuple-element.5.window_starts, bf16[640,2048]{1,0:T(8,128)(2,1)S(1)} %fusion.2.at_ref, bf16[512,768]{1,0:T(8,128)(2,1)S(1)} %broadcast_select_fusion.1.gt_ref, f32[640,3200]{1,0:T(8,128)} %sum_squares.7.refs_0_), custom_call_target="tpu_custom_call", output_to_operand_aliasing={{}: (3, {})} | custom-call | flops 2013265920 | bytes 2752512 | tf_op jit(solution)/shard_map/sum_squares/pallas_call | solution.py:135
  242.8 6.1 %sum_squares.9 = f32[640,3200]{1,0:T(8,128)} custom-call(s32[16]{0:T(128)S(1)} %get-tuple-element.5.window_starts, bf16[640,2048]{1,0:T(8,128)(2,1)S(1)} %fusion.2.at_ref, bf16[512,640]{1,0:T(8,128)(2,1)S(1)} %broadcast_select_fusion.2.gt_ref, f32[640,3200]{1,0:T(8,128)} %sum_squares.8.refs_0_), custom_call_target="tpu_custom_call", output_to_operand_aliasing={{}: (3, {})} | custom-call | flops 1677721600 | bytes 2293760 | tf_op jit(solution)/shard_map/sum_squares/pallas_call | solution.py:135
  (79 shorter events, 19.3 us)
Async XLA Ops:
  0.0 1.3 copy-start
  0.0 15.5 %copy-start.5 = (s32[16]{0:T(128)S(1)}, s32[16]{0:T(128)}, u32[]{:S(2)}) copy-start(s32[16]{0:T(128)} %param.9) | copy-start | bytes 196
  5.4 12.2 %collective-permute-start.2 = (bf16[128,640]{1,0:T(8,128)(2,1)S(1)}, bf16[128,640]{1,0:T(8,128)(2,1)S(1)}, u32[]{:S(2)}, u32[]{:S(2)}) collective-permute-start(bf16[128,640]{1,0:T(8,128)(2,1)S(1)} %convolution_convert_fusion), channel_id=1, source_target_pairs={{12,0},{1,5},{6,10},{11,15},{28,16},{17,21},{22,26},{27,31}} | collective-permute-start | bytes 491528 | tf_op jit(solution)/shard_map/ppermute | solution.py:192
  6.7 25.8 %collective-permute-start.1 = (bf16[128,640]{1,0:T(8,128)(2,1)S(1)}, bf16[128,640]{1,0:T(8,128)(2,1)}, u32[]{:S(2)}, u32[]{:S(2)}) collective-permute-start(bf16[128,640]{1,0:T(8,128)(2,1)S(1)} %convolution_convert_fusion), channel_id=1, source_target_pairs={{8,0},{13,5},{2,10},{7,15},{24,16},{29,21},{18,26},{23,31}} | collective-permute-start | bytes 491528 | tf_op jit(solution)/shard_map/ppermute | solution.py:192
  9.5 10.8 %collective-permute-start.13 = (bf16[32,3200]{1,0:T(8,128)(2,1)S(1)}, bf16[32,3200]{1,0:T(8,128)(2,1)S(1)}, u32[]{:S(2)}, u32[]{:S(2)}) collective-permute-start(bf16[32,3200]{1,0:T(8,128)(2,1)S(1)} %get-tuple-element.7), channel_id=1, source_target_pairs={{0,12},{4,0},{8,4},{12,8},{1,13},{5,1},{9,5},{13,9},{2,14},{6,2},{... | collective-permute-start | bytes 614408 | tf_op jit(solution)/shard_map/ppermute | solution.py:171
  11.6 20.9 %collective-permute-start.5 = (bf16[32,3200]{1,0:T(8,128)(2,1)S(1)}, bf16[32,3200]{1,0:T(8,128)(2,1)S(1)}, u32[]{:S(2)}, u32[]{:S(2)}) collective-permute-start(bf16[32,3200]{1,0:T(8,128)(2,1)S(1)} %get-tuple-element.8), channel_id=1, source_target_pairs={{0,8},{4,12},{8,0},{12,4},{1,9},{5,13},{9,1},{13,5},{2,10},{6,14},... | collective-permute-start | bytes 614408 | tf_op jit(solution)/shard_map/ppermute | solution.py:171
  13.2 20.8 %collective-permute-start.9 = (bf16[32,3200]{1,0:T(8,128)(2,1)S(1)}, bf16[32,3200]{1,0:T(8,128)(2,1)S(1)}, u32[]{:S(2)}, u32[]{:S(2)}) collective-permute-start(bf16[32,3200]{1,0:T(8,128)(2,1)S(1)} %get-tuple-element.9), channel_id=1, source_target_pairs={{0,4},{4,8},{8,12},{12,0},{1,5},{5,9},{9,13},{13,1},{2,6},{6,10},{... | collective-permute-start | bytes 614408 | tf_op jit(solution)/shard_map/ppermute | solution.py:171
  17.6 1.3 copy-start.3
  17.6 18.9 %collective-permute-start = (bf16[128,640]{1,0:T(8,128)(2,1)S(1)}, bf16[128,640]{1,0:T(8,128)(2,1)}, u32[]{:S(2)}, u32[]{:S(2)}) collective-permute-start(bf16[128,640]{1,0:T(8,128)(2,1)S(1)} %convolution_convert_fusion), channel_id=1, source_target_pairs={{4,0},{9,5},{14,10},{3,15},{20,16},{25,21},{30,26},{19,31}} | collective-permute-start | bytes 491528 | tf_op jit(solution)/shard_map/ppermute | solution.py:192
  20.3 16.2 %collective-permute-start.15 = (bf16[32,3200]{1,0:T(8,128)(2,1)S(1)}, bf16[32,3200]{1,0:T(8,128)(2,1)S(1)}, u32[]{:S(2)}, u32[]{:S(2)}) collective-permute-start(bf16[32,3200]{1,0:T(8,128)(2,1)S(1)} %collective-permute-done.13.refs_9_), channel_id=1, source_target_pairs={{0,1},{1,0},{2,3},{3,2},{4,5},{5,4},{6,7},{7,6},{8,9},{9,8},{10,11... | collective-permute-start | bytes 614408 | tf_op jit(solution)/shard_map/ppermute | solution.py:178
  32.5 6.7 %collective-permute-start.14 = (bf16[32,3200]{1,0:T(8,128)(2,1)S(1)}, bf16[32,3200]{1,0:T(8,128)(2,1)S(1)}, u32[]{:S(2)}, u32[]{:S(2)}) collective-permute-start(bf16[32,3200]{1,0:T(8,128)(2,1)S(1)} %collective-permute-done.13.refs_9_), channel_id=1, source_target_pairs={{0,2},{1,3},{2,0},{3,1},{4,6},{5,7},{6,4},{7,5},{8,10},{9,11},{10,... | collective-permute-start | bytes 614408 | tf_op jit(solution)/shard_map/ppermute | solution.py:174
  32.5 11.1 %collective-permute-start.6 = (bf16[32,3200]{1,0:T(8,128)(2,1)S(1)}, bf16[32,3200]{1,0:T(8,128)(2,1)S(1)}, u32[]{:S(2)}, u32[]{:S(2)}) collective-permute-start(bf16[32,3200]{1,0:T(8,128)(2,1)S(1)} %collective-permute-done.5.refs_1_), channel_id=1, source_target_pairs={{0,2},{1,3},{2,0},{3,1},{4,6},{5,7},{6,4},{7,5},{8,10},{9,11},{10,... | collective-permute-start | bytes 614408 | tf_op jit(solution)/shard_map/ppermute | solution.py:174
  34.0 14.0 %collective-permute-start.10 = (bf16[32,3200]{1,0:T(8,128)(2,1)S(1)}, bf16[32,3200]{1,0:T(8,128)(2,1)S(1)}, u32[]{:S(2)}, u32[]{:S(2)}) collective-permute-start(bf16[32,3200]{1,0:T(8,128)(2,1)S(1)} %collective-permute-done.9.refs_5_), channel_id=1, source_target_pairs={{0,2},{1,3},{2,0},{3,1},{4,6},{5,7},{6,4},{7,5},{8,10},{9,11},{10,... | collective-permute-start | bytes 614408 | tf_op jit(solution)/shard_map/ppermute | solution.py:174
  36.5 14.9 %collective-permute-start.7 = (bf16[32,3200]{1,0:T(8,128)(2,1)S(1)}, bf16[32,3200]{1,0:T(8,128)(2,1)S(1)}, u32[]{:S(2)}, u32[]{:S(2)}) collective-permute-start(bf16[32,3200]{1,0:T(8,128)(2,1)S(1)} %collective-permute-done.5.refs_1_), channel_id=1, source_target_pairs={{0,1},{1,0},{2,3},{3,2},{4,5},{5,4},{6,7},{7,6},{8,9},{9,8},{10,11... | collective-permute-start | bytes 614408 | tf_op jit(solution)/shard_map/ppermute | solution.py:178
  36.5 16.8 %collective-permute-start.11 = (bf16[32,3200]{1,0:T(8,128)(2,1)S(1)}, bf16[32,3200]{1,0:T(8,128)(2,1)S(1)}, u32[]{:S(2)}, u32[]{:S(2)}) collective-permute-start(bf16[32,3200]{1,0:T(8,128)(2,1)S(1)} %collective-permute-done.9.refs_5_), channel_id=1, source_target_pairs={{0,1},{1,0},{2,3},{3,2},{4,5},{5,4},{6,7},{7,6},{8,9},{9,8},{10,11... | collective-permute-start | bytes 614408 | tf_op jit(solution)/shard_map/ppermute | solution.py:178
  39.2 14.1 %collective-permute-start.16 = (bf16[32,3200]{1,0:T(8,128)(2,1)S(1)}, bf16[32,3200]{1,0:T(8,128)(2,1)S(1)}, u32[]{:S(2)}, u32[]{:S(2)}) collective-permute-start(bf16[32,3200]{1,0:T(8,128)(2,1)S(1)} %collective-permute-done.14.refs_10_), channel_id=1, source_target_pairs={{0,1},{1,0},{2,3},{3,2},{4,5},{5,4},{6,7},{7,6},{8,9},{9,8},{10,11... | collective-permute-start | bytes 614408 | tf_op jit(solution)/shard_map/ppermute | solution.py:178
  43.6 9.7 %collective-permute-start.8 = (bf16[32,3200]{1,0:T(8,128)(2,1)S(1)}, bf16[32,3200]{1,0:T(8,128)(2,1)S(1)}, u32[]{:S(2)}, u32[]{:S(2)}) collective-permute-start(bf16[32,3200]{1,0:T(8,128)(2,1)S(1)} %collective-permute-done.6.refs_2_), channel_id=1, source_target_pairs={{0,1},{1,0},{2,3},{3,2},{4,5},{5,4},{6,7},{7,6},{8,9},{9,8},{10,11... | collective-permute-start | bytes 614408 | tf_op jit(solution)/shard_map/ppermute | solution.py:178
  48.0 5.3 %collective-permute-start.12 = (bf16[32,3200]{1,0:T(8,128)(2,1)S(1)}, bf16[32,3200]{1,0:T(8,128)(2,1)S(1)}, u32[]{:S(2)}, u32[]{:S(2)}) collective-permute-start(bf16[32,3200]{1,0:T(8,128)(2,1)S(1)} %collective-permute-done.10.refs_6_), channel_id=1, source_target_pairs={{0,1},{1,0},{2,3},{3,2},{4,5},{5,4},{6,7},{7,6},{8,9},{9,8},{10,11... | collective-permute-start | bytes 614408 | tf_op jit(solution)/shard_map/ppermute | solution.py:178
  51.4 40.0 %collective-permute-start.3 = (bf16[512,640]{1,0:T(8,128)(2,1)S(1)}, bf16[512,640]{1,0:T(8,128)(2,1)S(1)}, u32[]{:S(2)}, u32[]{:S(2)}) collective-permute-start(bf16[512,640]{1,0:T(8,128)(2,1)S(1)} %pad_maximum_fusion), channel_id=1, source_target_pairs={{0,2},{5,7},{10,8},{15,13},{16,18},{21,23},{26,24},{31,29}} | collective-permute-start | bytes 1966088 | tf_op jit(solution)/shard_map/ppermute | solution.py:194
  62.1 1.9 copy-start.2
  72.6 21.2 %collective-permute-start.23 = (bf16[512,512]{1,0:T(8,128)(2,1)S(1)}, bf16[512,512]{1,0:T(8,128)(2,1)S(1)}, u32[]{:S(2)}, u32[]{:S(2)}) collective-permute-start(bf16[512,512]{1,0:T(8,128)(2,1)S(1)} %rotate_chunk.7), channel_id=1, source_target_pairs={{0,4},{12,8},{1,5},{13,9},{2,6},{14,10},{3,7},{15,11},{16,20},{28,... | collective-permute-start | bytes 1572872 | tf_op jit(solution)/shard_map/ppermute | solution.py:216
  82.5 10.2 %copy-start.4 = (bf16[128,640]{1,0:T(8,128)(2,1)S(1)}, bf16[128,640]{1,0:T(8,128)(2,1)}, u32[]{:S(2)}) copy-start(bf16[128,640]{1,0:T(8,128)(2,1)} %copy-done.3) | copy-start | bytes 491524
  82.5 17.1 %collective-permute-start.29 = (bf16[512,512]{1,0:T(8,128)(2,1)S(1)}, bf16[512,512]{1,0:T(8,128)(2,1)S(1)}, u32[]{:S(2)}, u32[]{:S(2)}) collective-permute-start(bf16[512,512]{1,0:T(8,128)(2,1)S(1)} %rotate_chunk.9), channel_id=1, source_target_pairs={{0,4},{12,8},{1,5},{13,9},{2,6},{14,10},{3,7},{15,11},{16,20},{28,... | collective-permute-start | bytes 1572872 | tf_op jit(solution)/shard_map/ppermute | solution.py:216
  88.8 24.9 %collective-permute-start.17 = (bf16[512,640]{1,0:T(8,128)(2,1)S(1)}, bf16[512,640]{1,0:T(8,128)(2,1)S(1)}, u32[]{:S(2)}, u32[]{:S(2)}) collective-permute-start(bf16[512,640]{1,0:T(8,128)(2,1)S(1)} %rotate_chunk.5), channel_id=1, source_target_pairs={{0,4},{12,8},{1,5},{13,9},{2,6},{14,10},{3,7},{15,11},{16,20},{28,... | collective-permute-start | bytes 1966088 | tf_op jit(solution)/shard_map/ppermute | solution.py:216
  90.1 40.5 %collective-permute-start.20 = (bf16[512,768]{1,0:T(8,128)(2,1)S(1)}, bf16[512,768]{1,0:T(8,128)(2,1)S(1)}, u32[]{:S(2)}, u32[]{:S(2)}) collective-permute-start(bf16[512,768]{1,0:T(8,128)(2,1)S(1)} %rotate_chunk.6), channel_id=1, source_target_pairs={{0,4},{12,8},{1,5},{13,9},{2,6},{14,10},{3,7},{15,11},{16,20},{28,... | collective-permute-start | bytes 2359304 | tf_op jit(solution)/shard_map/ppermute | solution.py:216
  91.4 55.3 %collective-permute-start.26 = (bf16[512,768]{1,0:T(8,128)(2,1)S(1)}, bf16[512,768]{1,0:T(8,128)(2,1)S(1)}, u32[]{:S(2)}, u32[]{:S(2)}) collective-permute-start(bf16[512,768]{1,0:T(8,128)(2,1)S(1)} %rotate_chunk.8), channel_id=1, source_target_pairs={{0,4},{12,8},{1,5},{13,9},{2,6},{14,10},{3,7},{15,11},{16,20},{28,... | collective-permute-start | bytes 2359304 | tf_op jit(solution)/shard_map/ppermute | solution.py:216
  93.9 54.9 %collective-permute-start.4 = (bf16[512,640]{1,0:T(8,128)(2,1)S(1)}, bf16[512,640]{1,0:T(8,128)(2,1)S(1)}, u32[]{:S(2)}, u32[]{:S(2)}) collective-permute-start(bf16[512,640]{1,0:T(8,128)(2,1)S(1)} %broadcast_select_fusion.3), channel_id=1, source_target_pairs={{0,1},{5,4},{10,11},{15,14},{2,3},{7,6},{8,9},{13,12},{16,17},{21,... | collective-permute-start | bytes 1966088 | tf_op jit(solution)/shard_map/ppermute | solution.py:196
  99.7 54.3 %collective-permute-start.24 = (bf16[512,512]{1,0:T(8,128)(2,1)S(1)}, bf16[512,512]{1,0:T(8,128)(2,1)S(1)}, u32[]{:S(2)}, u32[]{:S(2)}) collective-permute-start(bf16[512,512]{1,0:T(8,128)(2,1)S(1)} %add_convert_fusion.9), channel_id=1, source_target_pairs={{4,8},{8,4},{5,9},{9,5},{6,10},{10,6},{7,11},{11,7},{20,24},{24,20... | collective-permute-start | bytes 1572872 | tf_op jit(solution)/shard_map/ppermute | solution.py:217
  113.7 41.7 %collective-permute-start.30 = (bf16[512,512]{1,0:T(8,128)(2,1)S(1)}, bf16[512,512]{1,0:T(8,128)(2,1)S(1)}, u32[]{:S(2)}, u32[]{:S(2)}) collective-permute-start(bf16[512,512]{1,0:T(8,128)(2,1)S(1)} %add_convert_fusion.7), channel_id=1, source_target_pairs={{4,8},{8,4},{5,9},{9,5},{6,10},{10,6},{7,11},{11,7},{20,24},{24,20... | collective-permute-start | bytes 1572872 | tf_op jit(solution)/shard_map/ppermute | solution.py:217
  130.5 26.4 %collective-permute-start.18 = (bf16[512,640]{1,0:T(8,128)(2,1)S(1)}, bf16[512,640]{1,0:T(8,128)(2,1)S(1)}, u32[]{:S(2)}, u32[]{:S(2)}) collective-permute-start(bf16[512,640]{1,0:T(8,128)(2,1)S(1)} %add_convert_fusion.5), channel_id=1, source_target_pairs={{4,8},{8,4},{5,9},{9,5},{6,10},{10,6},{7,11},{11,7},{20,24},{24,20... | collective-permute-start | bytes 1966088 | tf_op jit(solution)/shard_map/ppermute | solution.py:217
  146.7 21.3 %collective-permute-start.21 = (bf16[512,768]{1,0:T(8,128)(2,1)S(1)}, bf16[512,768]{1,0:T(8,128)(2,1)S(1)}, u32[]{:S(2)}, u32[]{:S(2)}) collective-permute-start(bf16[512,768]{1,0:T(8,128)(2,1)S(1)} %add_convert_fusion.3), channel_id=1, source_target_pairs={{4,8},{8,4},{5,9},{9,5},{6,10},{10,6},{7,11},{11,7},{20,24},{24,20... | collective-permute-start | bytes 2359304 | tf_op jit(solution)/shard_map/ppermute | solution.py:217
  148.8 36.1 %collective-permute-start.27 = (bf16[512,768]{1,0:T(8,128)(2,1)S(1)}, bf16[512,768]{1,0:T(8,128)(2,1)S(1)}, u32[]{:S(2)}, u32[]{:S(2)}) collective-permute-start(bf16[512,768]{1,0:T(8,128)(2,1)S(1)} %add_convert_fusion.1), channel_id=1, source_target_pairs={{4,8},{8,4},{5,9},{9,5},{6,10},{10,6},{7,11},{11,7},{20,24},{24,20... | collective-permute-start | bytes 2359304 | tf_op jit(solution)/shard_map/ppermute | solution.py:217
  154.1 36.9 %collective-permute-start.25 = (bf16[512,512]{1,0:T(8,128)(2,1)S(1)}, bf16[512,512]{1,0:T(8,128)(2,1)S(1)}, u32[]{:S(2)}, u32[]{:S(2)}) collective-permute-start(bf16[512,512]{1,0:T(8,128)(2,1)S(1)} %add_convert_fusion.8), channel_id=1, source_target_pairs={{4,0},{8,12},{5,1},{9,13},{6,2},{10,14},{7,3},{11,15},{20,16},{24,... | collective-permute-start | bytes 1572872 | tf_op jit(solution)/shard_map/ppermute | solution.py:218
  155.6 30.8 %collective-permute-start.31 = (bf16[512,512]{1,0:T(8,128)(2,1)S(1)}, bf16[512,512]{1,0:T(8,128)(2,1)S(1)}, u32[]{:S(2)}, u32[]{:S(2)}) collective-permute-start(bf16[512,512]{1,0:T(8,128)(2,1)S(1)} %add_convert_fusion.6), channel_id=1, source_target_pairs={{4,0},{8,12},{5,1},{9,13},{6,2},{10,14},{7,3},{11,15},{20,16},{24,... | collective-permute-start | bytes 1572872 | tf_op jit(solution)/shard_map/ppermute | solution.py:218
  157.1 35.0 %collective-permute-start.19 = (bf16[512,640]{1,0:T(8,128)(2,1)S(1)}, bf16[512,640]{1,0:T(8,128)(2,1)S(1)}, u32[]{:S(2)}, u32[]{:S(2)}) collective-permute-start(bf16[512,640]{1,0:T(8,128)(2,1)S(1)} %add_convert_fusion.4), channel_id=1, source_target_pairs={{4,0},{8,12},{5,1},{9,13},{6,2},{10,14},{7,3},{11,15},{20,16},{24,... | collective-permute-start | bytes 1966088 | tf_op jit(solution)/shard_map/ppermute | solution.py:218
  168.2 68.4 %collective-permute-start.22 = (bf16[512,768]{1,0:T(8,128)(2,1)S(1)}, bf16[512,768]{1,0:T(8,128)(2,1)S(1)}, u32[]{:S(2)}, u32[]{:S(2)}) collective-permute-start(bf16[512,768]{1,0:T(8,128)(2,1)S(1)} %add_convert_fusion.2), channel_id=1, source_target_pairs={{4,0},{8,12},{5,1},{9,13},{6,2},{10,14},{7,3},{11,15},{20,16},{24,... | collective-permute-start | bytes 2359304 | tf_op jit(solution)/shard_map/ppermute | solution.py:218
  185.0 40.8 %collective-permute-start.28 = (bf16[512,768]{1,0:T(8,128)(2,1)S(1)}, bf16[512,768]{1,0:T(8,128)(2,1)S(1)}, u32[]{:S(2)}, u32[]{:S(2)}) collective-permute-start(bf16[512,768]{1,0:T(8,128)(2,1)S(1)} %add_convert_fusion), channel_id=1, source_target_pairs={{4,0},{8,12},{5,1},{9,13},{6,2},{10,14},{7,3},{11,15},{20,16},{24,... | collective-permute-start | bytes 2359304 | tf_op jit(solution)/shard_map/ppermute | solution.py:218
  242.8 6.1 %copy-start.1 = (bf16[128,5120]{1,0:T(8,128)(2,1)S(1)}, bf16[128,5120]{1,0:T(8,128)(2,1)}, u32[]{:S(2)}) copy-start(bf16[128,5120]{1,0:T(8,128)(2,1)} %param.5) | copy-start | bytes 3932164

commit v2 on v1

--- a/solution.py
+++ b/solution.py
@@ -22,7 +22,7 @@
     ]
 
 
-def compact_kernel(tgt, lim, pieces, *refs):
+def compact_kernel(pieces, place_ref, *refs):
     sources, out, buf, sems = refs[: len(pieces)], refs[-3], refs[-2], refs[-1]
     copies = []
     row = 0
@@ -30,12 +30,8 @@
         copies.append(pltpu.make_async_copy(sources[j], buf.at[pl.ds(row, size)], sems.at[j]))
         copies[-1].start()
         row += size
-    selectors = []
-    for j, size in enumerate(pieces):
-        place = lax.broadcasted_iota(jnp.int32, (out.shape[0], size), 0)
-        token = lax.broadcasted_iota(jnp.int32, (out.shape[0], size), 1) + tgt[j]
-        selectors.append(jnp.where((place == token) & (place < lim[j]), 1.0, 0.0))
-    selector = jnp.concatenate(selectors, axis=1).astype(jnp.bfloat16)
+    place = lax.broadcasted_iota(jnp.int32, (out.shape[0], row), 0)
+    selector = jnp.where(place == place_ref[...], 1.0, 0.0).astype(jnp.bfloat16)
     for copy in copies:
         copy.wait()
     width = out.shape[1]
@@ -46,29 +42,22 @@
         ).astype(out.dtype)
 
 
-def compact(pieces, targets, limits, rows):
+def compact(pieces, places, rows):
     sizes = tuple(p.shape[0] for p in pieces)
     width = pieces[0].shape[1]
-
-    def kernel(tgt, lim, *refs):
-        compact_kernel(tgt, lim, sizes, *refs)
-
     return pl.pallas_call(
-        kernel,
-        grid_spec=pltpu.PrefetchScalarGridSpec(
-            num_scalar_prefetch=2,
-            grid=(),
-            in_specs=[pl.BlockSpec(memory_space=pl.ANY)] * len(pieces),
-            out_specs=pl.BlockSpec(memory_space=pltpu.VMEM),
-            scratch_shapes=[
-                pltpu.VMEM((sum(sizes), width), jnp.bfloat16),
-                pltpu.SemaphoreType.DMA((len(pieces),)),
-            ],
-        ),
+        functools.partial(compact_kernel, sizes),
+        in_specs=[pl.BlockSpec(memory_space=pltpu.VMEM)]
+        + [pl.BlockSpec(memory_space=pl.ANY)] * len(pieces),
+        out_specs=pl.BlockSpec(memory_space=pltpu.VMEM),
+        scratch_shapes=[
+            pltpu.VMEM((sum(sizes), width), jnp.bfloat16),
+            pltpu.SemaphoreType.DMA((len(pieces),)),
+        ],
         out_shape=jax.ShapeDtypeStruct((rows, width), jnp.bfloat16),
         compiler_params=pltpu.CompilerParams(vmem_limit_bytes=VMEM_LIMIT),
         name="compact_rows",
-    )(targets, limits, *pieces)
+    )(places[None, :], *pieces)
 
 
 def rotate_kernel(rows_ref, basis_ref, out_ref):
@@ -165,9 +154,10 @@
         mine = lax.dynamic_slice_in_dim(gradients, m * share, share, 0)
         own = lax.dynamic_slice_in_dim(gradients, d * width, width, 1)
         pieces = [(own, d, 0)]
-        far = []
+        far, sent = [], []
         for k in (2, 1, 3):
             block = lax.dynamic_slice_in_dim(mine, lax.rem(d + k, shards) * width, width, 1)
+            sent.append(block)
             received = lax.ppermute(block, "dp", [(e, (e + k) % shards) for e in range(shards)])
             far.append((received, lax.rem(d + shards - k, shards)))
         for received, e in far:
@@ -177,9 +167,9 @@
             for piece, part in ((received, m ^ 1), (crossed, m ^ 3)):
                 swapped = lax.ppermute(piece, "mp", [(p, p ^ 1) for p in range(parts)])
                 pieces.append((swapped, e, part * share))
-        return pieces
+        return pieces, sent
     exchanged = lax.all_to_all(gradients, "dp", split_axis=1, concat_axis=0, tiled=True)
-    return [(exchanged[e * rows : (e + 1) * rows], e, 0) for e in range(shards)]
+    return [(exchanged[e * rows : (e + 1) * rows], e, 0) for e in range(shards)], []
 
 
 def exchange_inputs(rotated_in, shards, parts):
@@ -206,17 +196,30 @@
     return held, jnp.arange(shards, dtype=jnp.int32)
 
 
+def after(x, *others):
+    others = [o for o in others if o is not None]
+    return lax.optimization_barrier((x, *others))[0] if others else x
+
+
 def sum_over_shards(parts, shards):
     if shards != 4:
         return [lax.psum(part, "dp") for part in parts]
     d = lax.axis_index("dp")
     middle = (d == 1) | (d == 2)
-    sums = []
-    for part in parts:
-        pair = add_rounded(part, lax.ppermute(part, "dp", [(0, 1), (3, 2)]))
-        both = add_rounded(pair, lax.ppermute(pair, "dp", [(1, 2), (2, 1)]))
-        sums.append(jnp.where(middle, both, lax.ppermute(both, "dp", [(1, 0), (2, 3)])))
-    return sums
+    count = len(parts)
+    inward = [lax.ppermute(part, "dp", [(0, 1), (3, 2)]) for part in parts]
+    pairs, across, sums, outward, done = {}, {}, {}, {}, {}
+    for s in range(count + 2):
+        if s < count:
+            pairs[s] = add_rounded(parts[s], after(inward[s], sums.get(s - 2)))
+            across[s] = lax.ppermute(pairs[s], "dp", [(1, 2), (2, 1)])
+        if 1 <= s <= count:
+            sums[s - 1] = add_rounded(pairs[s - 1], after(across[s - 1], pairs.get(s)))
+            outward[s - 1] = lax.ppermute(sums[s - 1], "dp", [(1, 0), (2, 3)])
+        if s >= 2:
+            got = after(outward[s - 2], sums.get(s - 1))
+            done[s - 2] = jnp.where(middle, sums[s - 2], got)
+    return [done[c] for c in range(count)]
 
 
 def per_device(activations, gradients, input_basis, output_basis, lengths):
@@ -232,17 +235,20 @@
     shard_starts = seq_starts[::per_shard]
     window_starts = jnp.minimum(seq_starts // ALIGN * ALIGN, rows - WINDOW)
 
-    pieces = exchange_gradients(gradients, shards, parts)
+    pieces, sent = exchange_gradients(gradients, shards, parts)
+    activations = after(activations, *sent)
     rotated_in = jnp.dot(activations, input_basis, preferred_element_type=jnp.float32).astype(
         jnp.bfloat16
     )
     held, order = exchange_inputs(rotated_in, shards, parts)
 
-    piece_shards = jnp.stack([jnp.asarray(e, jnp.int32) for _, e, _ in pieces])
-    piece_rows = jnp.stack([jnp.asarray(r, jnp.int32) for _, _, r in pieces])
-    targets = shard_starts[piece_shards] + piece_rows
-    limits = shard_ends[piece_shards]
-    compacted = compact([p for p, _, _ in pieces], targets, limits, rows)
+    places = []
+    for piece, e, row in pieces:
+        start = lax.dynamic_index_in_dim(shard_starts, e, keepdims=False)
+        end = lax.dynamic_index_in_dim(shard_ends, e, keepdims=False)
+        place = start + row + jnp.arange(piece.shape[0], dtype=jnp.int32)
+        places.append(jnp.where(place < end, place, -1))
+    compacted = compact([p for p, _, _ in pieces], jnp.concatenate(places), rows)
 
     place = window_starts[:, None] + jnp.arange(WINDOW, dtype=jnp.int32)[None, :]
     inside = (place >= seq_starts[:, None]) & (place < seq_ends[:, None])
@@ -259,7 +265,10 @@
 
     width = output_basis.shape[1]
     chunks = column_chunks(width)
-    partials = [rotate(compacted, output_basis, first, size) for first, size in chunks]
+    partials = []
+    for first, size in chunks:
+        source = after(compacted, *partials[-1:])
+        partials.append(rotate(source, output_basis, first, size))
     result = None
     for (first, _), gt_chunk in zip(chunks, sum_over_shards(partials, shards)):
         result = squares(window_starts, at_windows, gt_chunk, 1.0 / rows, first, width, result)

time: 252 us -> 228 us (0.905)
  waiting for transfers between devices: 115 us -> 76.2 us
  other arithmetic: 4.57 us -> 16.8 us
  between operations: 0.56 us -> 8.04 us
  starting transfers between devices: 56.8 us -> 52.9 us
    ppermute x15, waiting for transfers between devices: 104 us -> 67.2 us  [the longest x5 25.7 us: sum_over_shards(): across[s] = lax.ppermute(pairs[s], 'dp', [(1, 2), (2, 1)])]
    select_n x6 -> x18, other arithmetic: 0.35 us -> 14 us  [the longest x13 13.7 us: per_device(): places.append(jnp.where(place < end, place, -1))]
    ppermute x6, starting transfers between devices: 15.8 us -> 6.08 us  [exchange_gradients(): swapped = lax.ppermute(piece, 'mp', [(p, p ^ 1) for p in range(parts)])]
    ppermute x15, starting transfers between devices: 24.4 us -> 30.4 us  [the longest x5 14.6 us: sum_over_shards(): across[s] = lax.ppermute(pairs[s], 'dp', [(1, 2), (2, 1)])]
  transfers between devices with their start and end apart: 32 -> 32, of which waited for: 13 -> 12; matrix products, arithmetic and copies ran while one was open for 4% -> 12% of each run, Pallas kernels for 18% -> 20%
where the time goes in v2:
time: 228 us; the launch traced here: 224 us
  waiting for transfers between devices  76.2 us (33%)
  Pallas kernels  56.7 us (25%)
  starting transfers between devices  52.9 us (23%)
  other arithmetic  16.8 us (7%)
  between operations  8.04 us (4%)
  local copies, waits for them, and re-layouts  7.19 us (3%)
  matrix products  5.8 us (3%)
    pallas_call x5, Pallas kernels, squares(): pl.pallas_call(functools.partial(squares_kernel, seqs, scale), grid_spec=...  27.3 us
    ppermute x5, waiting for transfers between devices, sum_over_shards(): across[s] = lax.ppermute(pairs[s], 'dp', [(1, 2), (2, 1)])  25.7 us
    ppermute x5, waiting for transfers between devices, sum_over_shards(): outward[s - 1] = lax.ppermute(sums[s - 1], 'dp', [(1, 0), (2, 3)])  24.7 us
    pallas_call x5, Pallas kernels, rotate(): pl.pallas_call(rotate_kernel, grid=(-(-size // TILE),), in_specs=[pl.Bloc...  22 us
    ppermute x5, waiting for transfers between devices, sum_over_shards(): inward = [lax.ppermute(part, 'dp', [(0, 1), (3, 2)]) for part in parts]  16.9 us
    ppermute x5, starting transfers between devices, sum_over_shards(): across[s] = lax.ppermute(pairs[s], 'dp', [(1, 2), (2, 1)])  14.6 us
    select_n x13, other arithmetic, per_device(): places.append(jnp.where(place < end, place, -1))  13.7 us
    ppermute x5, starting transfers between devices, sum_over_shards(): outward[s - 1] = lax.ppermute(sums[s - 1], 'dp', [(1, 0), (2, 3)])  9.35 us
  transfers between devices with their start and end apart: 32, of which 12 were waited for; matrix products, arithmetic and copies ran while one was open for 12% of the time, Pallas kernels for 20%

profile of v2, /device:TPU:13, one launch (start us, length us, event | category | flops | bytes accessed | tf_op | source)
XLA Modules:
  0.0 223.7 jit_solution(1819214604023210915)
XLA Ops:
  0.0 1.5 fusion.15
  3.0 4.1 %collective-permute-start.5 = (bf16[32,3200]{1,0:T(8,128)(2,1)S(1)}, bf16[32,3200]{1,0:T(8,128)(2,1)S(1)}, u32[]{:S(2)}, u32[]{:S(2)}) collective-permute-start(bf16[32,3200]{1,0:T(8,128)(2,1)S(1)} %get-tuple-element.41), channel_id=1, source_target_pairs={{0,8},{4,12},{8,0},{12,4},{1,9},{5,13},{9,1},{13,5},{2,10},{6,14},... | collective-permute-start | bytes 614408 | tf_op jit(solution)/shard_map/ppermute | solution.py:161
  30.5 1.7 compare_select_fusion.12
  32.2 4.1 %convolution_convert_fusion = bf16[128,640]{1,0:T(8,128)(2,1)S(1)} fusion(bf16[128,5120]{1,0:T(8,128)(2,1)S(1)} %copy-done, bf16[5120,640]{1,0:T(8,128)(2,1)} %param.7), kind=kOutput, calls=%fused_computation.11 | convolution fusion | flops 838942720 | bytes 8028160 | tf_op jit(solution)/shard_map/dot_general | solution.py:240
  37.0 1.6 collective-permute-start.15
  42.5 2.8 %collective-permute-done.14.refs_10_ = bf16[32,3200]{1,0:T(8,128)(2,1)S(1)} collective-permute-done((bf16[32,3200]{1,0:T(8,128)(2,1)S(1)}, bf16[32,3200]{1,0:T(8,128)(2,1)S(1)}, u32[]{:S(2)}, u32[]{:S(2)}) %collective-permute-start.14) | collective-permute-done | bytes 204832 | tf_op jit(solution)/shard_map/ppermute | solution.py:164
  45.3 1.3 collective-permute-start.16
  46.6 3.1 %collective-permute-done.10.refs_6_ = bf16[32,3200]{1,0:T(8,128)(2,1)S(1)} collective-permute-done((bf16[32,3200]{1,0:T(8,128)(2,1)S(1)}, bf16[32,3200]{1,0:T(8,128)(2,1)S(1)}, u32[]{:S(2)}, u32[]{:S(2)}) %collective-permute-start.10) | collective-permute-done | bytes 204832 | tf_op jit(solution)/shard_map/ppermute | solution.py:164
  49.7 1.3 collective-permute-start.12
  51.0 3.1 %collective-permute-done.6.refs_2_ = bf16[32,3200]{1,0:T(8,128)(2,1)S(1)} collective-permute-done((bf16[32,3200]{1,0:T(8,128)(2,1)S(1)}, bf16[32,3200]{1,0:T(8,128)(2,1)S(1)}, u32[]{:S(2)}, u32[]{:S(2)}) %collective-permute-start.6) | collective-permute-done | bytes 204832 | tf_op jit(solution)/shard_map/ppermute | solution.py:164
  56.3 1.3 collective-permute-start.1
  57.6 1.3 collective-permute-start
  58.9 7.4 %compact_rows.1.rows_ref = bf16[512,3200]{1,0:T(8,128)(2,1)} custom-call(s32[1,512]{1,0:T(1,128)S(1)} %bitcast.16, bf16[128,3200]{1,0:T(8,128)(2,1)S(1)} %constant_dynamic-slice_fusion.refs_0_, bf16[32,3200]{1,0:T(8,128)(2,1)S(1)} %collective-permute-done.5.refs_1_, bf16[32,3200]{1,0:T(8,128)(2,1)S(1)} %collective-permute-done.6.refs_2_, ...), custom_call_target="tpu_custom_call" | custom-call | tf_op jit(solution)/shard_map/compact_rows/pallas_call | solution.py:48
  66.4 1.9 copy-done.2
  68.3 3.6 %rotate_chunk.5 = bf16[512,512]{1,0:T(8,128)(2,1)S(1)} custom-call(bf16[512,3200]{1,0:T(8,128)(2,1)S(1)} %copy-done.2, bf16[3200,3200]{1,0:T(8,128)(2,1)} %basis_ref.9), custom_call_target="tpu_custom_call" | custom-call | flops 1677721600 | bytes 6553600 | tf_op jit(solution)/shard_map/rotate_chunk/pallas_call | solution.py:72
  71.9 1.3 collective-permute-start.19
  73.2 5.0 %rotate_chunk.6 = bf16[512,768]{1,0:T(8,128)(2,1)S(1)} custom-call(bf16[512,3200]{1,0:T(8,128)(2,1)S(1)} %copy-done.2, bf16[3200,3200]{1,0:T(8,128)(2,1)} %basis_ref.9), custom_call_target="tpu_custom_call" | custom-call | flops 2516582400 | bytes 8192000 | tf_op jit(solution)/shard_map/rotate_chunk/pallas_call | solution.py:72
  79.6 2.9 %collective-permute-start.3 = (bf16[512,640]{1,0:T(8,128)(2,1)S(1)}, bf16[512,640]{1,0:T(8,128)(2,1)S(1)}, u32[]{:S(2)}, u32[]{:S(2)}) collective-permute-start(bf16[512,640]{1,0:T(8,128)(2,1)S(1)} %pad_maximum_fusion), channel_id=1, source_target_pairs={{0,2},{5,7},{10,8},{15,13},{16,18},{21,23},{26,24},{31,29}} | collective-permute-start | bytes 1966088 | tf_op jit(solution)/shard_map/ppermute | solution.py:184
  82.5 3.6 %rotate_chunk.7 = bf16[512,512]{1,0:T(8,128)(2,1)S(1)} custom-call(bf16[512,3200]{1,0:T(8,128)(2,1)S(1)} %copy-done.2, bf16[3200,3200]{1,0:T(8,128)(2,1)} %basis_ref.9), custom_call_target="tpu_custom_call" | custom-call | flops 1677721600 | bytes 6553600 | tf_op jit(solution)/shard_map/rotate_chunk/pallas_call | solution.py:72
  87.4 5.0 %rotate_chunk.8 = bf16[512,768]{1,0:T(8,128)(2,1)S(1)} custom-call(bf16[512,3200]{1,0:T(8,128)(2,1)S(1)} %copy-done.2, bf16[3200,3200]{1,0:T(8,128)(2,1)} %basis_ref.9), custom_call_target="tpu_custom_call" | custom-call | flops 2516582400 | bytes 8192000 | tf_op jit(solution)/shard_map/rotate_chunk/pallas_call | solution.py:72
  93.9 1.9 collective-permute-start.20
  95.8 8.8 %collective-permute-done.21 = bf16[512,768]{1,0:T(8,128)(2,1)S(1)} collective-permute-done((bf16[512,768]{1,0:T(8,128)(2,1)S(1)}, bf16[512,768]{1,0:T(8,128)(2,1)S(1)}, u32[]{:S(2)}, u32[]{:S(2)}) %collective-permute-start.21) | collective-permute-done | bytes 786464 | tf_op jit(solution)/shard_map/ppermute | solution.py:210
  104.7 4.1 %collective-permute-start.24 = (bf16[512,768]{1,0:T(8,128)(2,1)S(1)}, bf16[512,768]{1,0:T(8,128)(2,1)S(1)}, u32[]{:S(2)}, u32[]{:S(2)}) collective-permute-start(bf16[512,768]{1,0:T(8,128)(2,1)S(1)} %add_convert_fusion.3), channel_id=1, source_target_pairs={{4,8},{8,4},{5,9},{9,5},{6,10},{10,6},{7,11},{11,7},{20,24},{24,20... | collective-permute-start | bytes 2359304 | tf_op jit(solution)/shard_map/ppermute | solution.py:215
  108.8 4.8 %rotate_chunk.9 = bf16[512,640]{1,0:T(8,128)(2,1)S(1)} custom-call(bf16[512,3200]{1,0:T(8,128)(2,1)S(1)} %copy-done.2, bf16[3200,3200]{1,0:T(8,128)(2,1)} %basis_ref.9), custom_call_target="tpu_custom_call" | custom-call | flops 2097152000 | bytes 7372800 | tf_op jit(solution)/shard_map/rotate_chunk/pallas_call | solution.py:72
  113.6 1.3 collective-permute-start.17
  115.1 1.3 collective-permute-start.4
  116.6 4.0 %collective-permute-start.31 = (bf16[512,512]{1,0:T(8,128)(2,1)S(1)}, bf16[512,512]{1,0:T(8,128)(2,1)S(1)}, u32[]{:S(2)}, u32[]{:S(2)}) collective-permute-start(bf16[512,512]{1,0:T(8,128)(2,1)S(1)} %add_convert_fusion.8), channel_id=1, source_target_pairs={{4,0},{8,12},{5,1},{9,13},{6,2},{10,14},{7,3},{11,15},{20,16},{24,... | collective-permute-start | bytes 1572872 | tf_op jit(solution)/shard_map/ppermute | solution.py:218
  120.8 5.8 %collective-permute-done.24 = bf16[512,768]{1,0:T(8,128)(2,1)S(1)} collective-permute-done((bf16[512,768]{1,0:T(8,128)(2,1)S(1)}, bf16[512,768]{1,0:T(8,128)(2,1)S(1)}, u32[]{:S(2)}, u32[]{:S(2)}) %collective-permute-start.24) | collective-permute-done | bytes 786464 | tf_op jit(solution)/shard_map/ppermute | solution.py:215
  126.6 2.1 collective-permute-start.22
  128.9 3.7 %collective-permute-done.23 = bf16[512,768]{1,0:T(8,128)(2,1)S(1)} collective-permute-done((bf16[512,768]{1,0:T(8,128)(2,1)S(1)}, bf16[512,768]{1,0:T(8,128)(2,1)S(1)}, u32[]{:S(2)}, u32[]{:S(2)}) %collective-permute-start.23) | collective-permute-done | bytes 786464 | tf_op jit(solution)/shard_map/ppermute | solution.py:210
  132.8 4.1 %collective-permute-start.27 = (bf16[512,768]{1,0:T(8,128)(2,1)S(1)}, bf16[512,768]{1,0:T(8,128)(2,1)S(1)}, u32[]{:S(2)}, u32[]{:S(2)}) collective-permute-start(bf16[512,768]{1,0:T(8,128)(2,1)S(1)} %add_convert_fusion.1), channel_id=1, source_target_pairs={{4,8},{8,4},{5,9},{9,5},{6,10},{10,6},{7,11},{11,7},{20,24},{24,20... | collective-permute-start | bytes 2359304 | tf_op jit(solution)/shard_map/ppermute | solution.py:215
  136.9 5.1 %collective-permute-done.22 = bf16[512,512]{1,0:T(8,128)(2,1)S(1)} collective-permute-done((bf16[512,512]{1,0:T(8,128)(2,1)S(1)}, bf16[512,512]{1,0:T(8,128)(2,1)S(1)}, u32[]{:S(2)}, u32[]{:S(2)}) %collective-permute-start.22) | collective-permute-done | bytes 524320 | tf_op jit(solution)/shard_map/ppermute | solution.py:215
  142.1 4.3 %collective-permute-done.17 = bf16[512,640]{1,0:T(8,128)(2,1)S(1)} collective-permute-done((bf16[512,640]{1,0:T(8,128)(2,1)S(1)}, bf16[512,640]{1,0:T(8,128)(2,1)S(1)}, u32[]{:S(2)}, u32[]{:S(2)}) %collective-permute-start.17) | collective-permute-done | bytes 655392 | tf_op jit(solution)/shard_map/ppermute | solution.py:210
  146.6 2.5 %collective-permute-start.25 = (bf16[512,640]{1,0:T(8,128)(2,1)S(1)}, bf16[512,640]{1,0:T(8,128)(2,1)S(1)}, u32[]{:S(2)}, u32[]{:S(2)}) collective-permute-start(bf16[512,640]{1,0:T(8,128)(2,1)S(1)} %add_convert_fusion.5), channel_id=1, source_target_pairs={{4,8},{8,4},{5,9},{9,5},{6,10},{10,6},{7,11},{11,7},{20,24},{24,20... | collective-permute-start | bytes 1966088 | tf_op jit(solution)/shard_map/ppermute | solution.py:215
  149.1 1.7 fusion.2.at_ref
  150.9 1.3 collective-permute-start.30
  152.2 1.3 collective-permute-start.29
  153.6 4.5 %sum_squares.5.refs_0_ = f32[640,3200]{1,0:T(8,128)} custom-call(s32[16]{0:T(128)S(1)} %get-tuple-element.37.window_starts, bf16[640,2048]{1,0:T(8,128)(2,1)S(1)} %fusion.2.at_ref, bf16[512,512]{1,0:T(8,128)(2,1)S(1)} %broadcast_select_fusion.4.gt_ref), custom_call_target="tpu_custom_call" | custom-call | flops 1342177280 | bytes 1835008 | tf_op jit(solution)/shard_map/sum_squares/pallas_call | solution.py:124
  158.2 14.7 %collective-permute-done.25 = bf16[512,640]{1,0:T(8,128)(2,1)S(1)} collective-permute-done((bf16[512,640]{1,0:T(8,128)(2,1)S(1)}, bf16[512,640]{1,0:T(8,128)(2,1)S(1)}, u32[]{:S(2)}, u32[]{:S(2)}) %collective-permute-start.25) | collective-permute-done | bytes 655392 | tf_op jit(solution)/shard_map/ppermute | solution.py:215
  173.0 1.3 collective-permute-start.26
  174.6 1.3 collective-permute-start.28
  176.0 4.7 %collective-permute-done.29 = bf16[512,512]{1,0:T(8,128)(2,1)S(1)} collective-permute-done((bf16[512,512]{1,0:T(8,128)(2,1)S(1)}, bf16[512,512]{1,0:T(8,128)(2,1)S(1)}, u32[]{:S(2)}, u32[]{:S(2)}) %collective-permute-start.29) | collective-permute-done | bytes 524320 | tf_op jit(solution)/shard_map/ppermute | solution.py:218
  180.8 6.1 %sum_squares.6.refs_0_ = f32[640,3200]{1,0:T(8,128)} custom-call(s32[16]{0:T(128)S(1)} %get-tuple-element.37.window_starts, bf16[640,2048]{1,0:T(8,128)(2,1)S(1)} %fusion.2.at_ref, bf16[512,768]{1,0:T(8,128)(2,1)S(1)} %broadcast_select_fusion.gt_ref, f32[640,3200]{1,0:T(8,128)} %sum_squares.5.refs_0_), custom_call_target="tpu_custom_call", output_to_operand_aliasing={{}: (3, {})} | custom-call | flops 2013265920 | bytes 2752512 | tf_op jit(solution)/shard_map/sum_squares/pallas_call | solution.py:124
  186.9 4.5 %sum_squares.7.refs_0_ = f32[640,3200]{1,0:T(8,128)} custom-call(s32[16]{0:T(128)S(1)} %get-tuple-element.37.window_starts, bf16[640,2048]{1,0:T(8,128)(2,1)S(1)} %fusion.2.at_ref, bf16[512,512]{1,0:T(8,128)(2,1)S(1)} %broadcast_select_fusion.5.gt_ref, f32[640,3200]{1,0:T(8,128)} %sum_squares.6.refs_0_), custom_call_target="tpu_custom_call", output_to_operand_aliasing={{}: (3, {})} | custom-call | flops 1342177280 | bytes 1835008 | tf_op jit(solution)/shard_map/sum_squares/pallas_call | solution.py:124
  191.4 3.4 %collective-permute-done.26 = bf16[512,640]{1,0:T(8,128)(2,1)S(1)} collective-permute-done((bf16[512,640]{1,0:T(8,128)(2,1)S(1)}, bf16[512,640]{1,0:T(8,128)(2,1)S(1)}, u32[]{:S(2)}, u32[]{:S(2)}) %collective-permute-start.26) | collective-permute-done | bytes 655392 | tf_op jit(solution)/shard_map/ppermute | solution.py:218
  194.9 16.6 %collective-permute-done.28 = bf16[512,768]{1,0:T(8,128)(2,1)S(1)} collective-permute-done((bf16[512,768]{1,0:T(8,128)(2,1)S(1)}, bf16[512,768]{1,0:T(8,128)(2,1)S(1)}, u32[]{:S(2)}, u32[]{:S(2)}) %collective-permute-start.28) | collective-permute-done | bytes 786464 | tf_op jit(solution)/shard_map/ppermute | solution.py:218
  211.5 6.1 %sum_squares.8.refs_0_ = f32[640,3200]{1,0:T(8,128)} custom-call(s32[16]{0:T(128)S(1)} %get-tuple-element.37.window_starts, bf16[640,2048]{1,0:T(8,128)(2,1)S(1)} %fusion.2.at_ref, bf16[512,768]{1,0:T(8,128)(2,1)S(1)} %broadcast_select_fusion.1.gt_ref, f32[640,3200]{1,0:T(8,128)} %sum_squares.7.refs_0_), custom_call_target="tpu_custom_call", output_to_operand_aliasing={{}: (3, {})} | custom-call | flops 2013265920 | bytes 2752512 | tf_op jit(solution)/shard_map/sum_squares/pallas_call | solution.py:124
  217.6 6.0 %sum_squares.9 = f32[640,3200]{1,0:T(8,128)} custom-call(s32[16]{0:T(128)S(1)} %get-tuple-element.37.window_starts, bf16[640,2048]{1,0:T(8,128)(2,1)S(1)} %fusion.2.at_ref, bf16[512,640]{1,0:T(8,128)(2,1)S(1)} %broadcast_select_fusion.2.gt_ref, f32[640,3200]{1,0:T(8,128)} %sum_squares.8.refs_0_), custom_call_target="tpu_custom_call", output_to_operand_aliasing={{}: (3, {})} | custom-call | flops 1677721600 | bytes 2293760 | tf_op jit(solution)/shard_map/sum_squares/pallas_call | solution.py:124
  (81 shorter events, 30.2 us)
Async XLA Ops:
  0.0 32.2 %copy-start = (bf16[128,5120]{1,0:T(8,128)(2,1)S(1)}, bf16[128,5120]{1,0:T(8,128)(2,1)}, u32[]{:S(2)}) copy-start(bf16[128,5120]{1,0:T(8,128)(2,1)} %param.5) | copy-start | bytes 3932164
  1.5 35.5 %collective-permute-start.13 = (bf16[32,3200]{1,0:T(8,128)(2,1)S(1)}, bf16[32,3200]{1,0:T(8,128)(2,1)S(1)}, u32[]{:S(2)}, u32[]{:S(2)}) collective-permute-start(bf16[32,3200]{1,0:T(8,128)(2,1)S(1)} %get-tuple-element.39), channel_id=1, source_target_pairs={{0,12},{4,0},{8,4},{12,8},{1,13},{5,1},{9,5},{13,9},{2,14},{6,2},{... | collective-permute-start | bytes 614408 | tf_op jit(solution)/shard_map/ppermute | solution.py:161
  1.8 38.1 %collective-permute-start.9 = (bf16[32,3200]{1,0:T(8,128)(2,1)S(1)}, bf16[32,3200]{1,0:T(8,128)(2,1)S(1)}, u32[]{:S(2)}, u32[]{:S(2)}) collective-permute-start(bf16[32,3200]{1,0:T(8,128)(2,1)S(1)} %get-tuple-element.40), channel_id=1, source_target_pairs={{0,4},{4,8},{8,12},{12,0},{1,5},{5,9},{9,13},{13,1},{2,6},{6,10},{... | collective-permute-start | bytes 614408 | tf_op jit(solution)/shard_map/ppermute | solution.py:161
  3.0 37.1 %collective-permute-start.5 = (bf16[32,3200]{1,0:T(8,128)(2,1)S(1)}, bf16[32,3200]{1,0:T(8,128)(2,1)S(1)}, u32[]{:S(2)}, u32[]{:S(2)}) collective-permute-start(bf16[32,3200]{1,0:T(8,128)(2,1)S(1)} %get-tuple-element.41), channel_id=1, source_target_pairs={{0,8},{4,12},{8,0},{12,4},{1,9},{5,13},{9,1},{13,5},{2,10},{6,14},... | collective-permute-start | bytes 614408 | tf_op jit(solution)/shard_map/ppermute | solution.py:161
  37.0 5.3 %collective-permute-start.15 = (bf16[32,3200]{1,0:T(8,128)(2,1)S(1)}, bf16[32,3200]{1,0:T(8,128)(2,1)S(1)}, u32[]{:S(2)}, u32[]{:S(2)}) collective-permute-start(bf16[32,3200]{1,0:T(8,128)(2,1)S(1)} %collective-permute-done.13.refs_9_), channel_id=1, source_target_pairs={{0,1},{1,0},{2,3},{3,2},{4,5},{5,4},{6,7},{7,6},{8,9},{9,8},{10,11... | collective-permute-start | bytes 614408 | tf_op jit(solution)/shard_map/ppermute | solution.py:168
  38.6 6.7 %collective-permute-start.14 = (bf16[32,3200]{1,0:T(8,128)(2,1)S(1)}, bf16[32,3200]{1,0:T(8,128)(2,1)S(1)}, u32[]{:S(2)}, u32[]{:S(2)}) collective-permute-start(bf16[32,3200]{1,0:T(8,128)(2,1)S(1)} %collective-permute-done.13.refs_9_), channel_id=1, source_target_pairs={{0,2},{1,3},{2,0},{3,1},{4,6},{5,7},{6,4},{7,5},{8,10},{9,11},{10,... | collective-permute-start | bytes 614408 | tf_op jit(solution)/shard_map/ppermute | solution.py:164
  39.9 9.8 %collective-permute-start.10 = (bf16[32,3200]{1,0:T(8,128)(2,1)S(1)}, bf16[32,3200]{1,0:T(8,128)(2,1)S(1)}, u32[]{:S(2)}, u32[]{:S(2)}) collective-permute-start(bf16[32,3200]{1,0:T(8,128)(2,1)S(1)} %collective-permute-done.9.refs_5_), channel_id=1, source_target_pairs={{0,2},{1,3},{2,0},{3,1},{4,6},{5,7},{6,4},{7,5},{8,10},{9,11},{10,... | collective-permute-start | bytes 614408 | tf_op jit(solution)/shard_map/ppermute | solution.py:164
  40.1 13.9 %collective-permute-start.6 = (bf16[32,3200]{1,0:T(8,128)(2,1)S(1)}, bf16[32,3200]{1,0:T(8,128)(2,1)S(1)}, u32[]{:S(2)}, u32[]{:S(2)}) collective-permute-start(bf16[32,3200]{1,0:T(8,128)(2,1)S(1)} %collective-permute-done.5.refs_1_), channel_id=1, source_target_pairs={{0,2},{1,3},{2,0},{3,1},{4,6},{5,7},{6,4},{7,5},{8,10},{9,11},{10,... | collective-permute-start | bytes 614408 | tf_op jit(solution)/shard_map/ppermute | solution.py:164
  41.4 13.6 %collective-permute-start.11 = (bf16[32,3200]{1,0:T(8,128)(2,1)S(1)}, bf16[32,3200]{1,0:T(8,128)(2,1)S(1)}, u32[]{:S(2)}, u32[]{:S(2)}) collective-permute-start(bf16[32,3200]{1,0:T(8,128)(2,1)S(1)} %collective-permute-done.9.refs_5_), channel_id=1, source_target_pairs={{0,1},{1,0},{2,3},{3,2},{4,5},{5,4},{6,7},{7,6},{8,9},{9,8},{10,11... | collective-permute-start | bytes 614408 | tf_op jit(solution)/shard_map/ppermute | solution.py:168
  42.4 13.9 %collective-permute-start.7 = (bf16[32,3200]{1,0:T(8,128)(2,1)S(1)}, bf16[32,3200]{1,0:T(8,128)(2,1)S(1)}, u32[]{:S(2)}, u32[]{:S(2)}) collective-permute-start(bf16[32,3200]{1,0:T(8,128)(2,1)S(1)} %collective-permute-done.5.refs_1_), channel_id=1, source_target_pairs={{0,1},{1,0},{2,3},{3,2},{4,5},{5,4},{6,7},{7,6},{8,9},{9,8},{10,11... | collective-permute-start | bytes 614408 | tf_op jit(solution)/shard_map/ppermute | solution.py:168
  45.3 12.3 %collective-permute-start.16 = (bf16[32,3200]{1,0:T(8,128)(2,1)S(1)}, bf16[32,3200]{1,0:T(8,128)(2,1)S(1)}, u32[]{:S(2)}, u32[]{:S(2)}) collective-permute-start(bf16[32,3200]{1,0:T(8,128)(2,1)S(1)} %collective-permute-done.14.refs_10_), channel_id=1, source_target_pairs={{0,1},{1,0},{2,3},{3,2},{4,5},{5,4},{6,7},{7,6},{8,9},{9,8},{10,11... | collective-permute-start | bytes 614408 | tf_op jit(solution)/shard_map/ppermute | solution.py:168
  49.7 9.2 %collective-permute-start.12 = (bf16[32,3200]{1,0:T(8,128)(2,1)S(1)}, bf16[32,3200]{1,0:T(8,128)(2,1)S(1)}, u32[]{:S(2)}, u32[]{:S(2)}) collective-permute-start(bf16[32,3200]{1,0:T(8,128)(2,1)S(1)} %collective-permute-done.10.refs_6_), channel_id=1, source_target_pairs={{0,1},{1,0},{2,3},{3,2},{4,5},{5,4},{6,7},{7,6},{8,9},{9,8},{10,11... | collective-permute-start | bytes 614408 | tf_op jit(solution)/shard_map/ppermute | solution.py:168
  54.1 4.8 %collective-permute-start.8 = (bf16[32,3200]{1,0:T(8,128)(2,1)S(1)}, bf16[32,3200]{1,0:T(8,128)(2,1)S(1)}, u32[]{:S(2)}, u32[]{:S(2)}) collective-permute-start(bf16[32,3200]{1,0:T(8,128)(2,1)S(1)} %collective-permute-done.6.refs_2_), channel_id=1, source_target_pairs={{0,1},{1,0},{2,3},{3,2},{4,5},{5,4},{6,7},{7,6},{8,9},{9,8},{10,11... | collective-permute-start | bytes 614408 | tf_op jit(solution)/shard_map/ppermute | solution.py:168
  55.0 24.5 %collective-permute-start.2 = (bf16[128,640]{1,0:T(8,128)(2,1)S(1)}, bf16[128,640]{1,0:T(8,128)(2,1)S(1)}, u32[]{:S(2)}, u32[]{:S(2)}) collective-permute-start(bf16[128,640]{1,0:T(8,128)(2,1)S(1)} %convolution_convert_fusion), channel_id=1, source_target_pairs={{12,0},{1,5},{6,10},{11,15},{28,16},{17,21},{22,26},{27,31}} | collective-permute-start | bytes 491528 | tf_op jit(solution)/shard_map/ppermute | solution.py:182
  56.3 23.2 %collective-permute-start.1 = (bf16[128,640]{1,0:T(8,128)(2,1)S(1)}, bf16[128,640]{1,0:T(8,128)(2,1)S(1)}, u32[]{:S(2)}, u32[]{:S(2)}) collective-permute-start(bf16[128,640]{1,0:T(8,128)(2,1)S(1)} %convolution_convert_fusion), channel_id=1, source_target_pairs={{8,0},{13,5},{2,10},{7,15},{24,16},{29,21},{18,26},{23,31}} | collective-permute-start | bytes 491528 | tf_op jit(solution)/shard_map/ppermute | solution.py:182
  57.6 21.9 %collective-permute-start = (bf16[128,640]{1,0:T(8,128)(2,1)S(1)}, bf16[128,640]{1,0:T(8,128)(2,1)S(1)}, u32[]{:S(2)}, u32[]{:S(2)}) collective-permute-start(bf16[128,640]{1,0:T(8,128)(2,1)S(1)} %convolution_convert_fusion), channel_id=1, source_target_pairs={{4,0},{9,5},{14,10},{3,15},{20,16},{25,21},{30,26},{19,31}} | collective-permute-start | bytes 491528 | tf_op jit(solution)/shard_map/ppermute | solution.py:182
  66.4 1.9 copy-start.2
  71.9 21.8 %collective-permute-start.19 = (bf16[512,512]{1,0:T(8,128)(2,1)S(1)}, bf16[512,512]{1,0:T(8,128)(2,1)S(1)}, u32[]{:S(2)}, u32[]{:S(2)}) collective-permute-start(bf16[512,512]{1,0:T(8,128)(2,1)S(1)} %rotate_chunk.5), channel_id=1, source_target_pairs={{0,4},{12,8},{1,5},{13,9},{2,6},{14,10},{3,7},{15,11},{16,20},{28,... | collective-permute-start | bytes 1572872 | tf_op jit(solution)/shard_map/ppermute | solution.py:210
  78.2 26.4 %collective-permute-start.21 = (bf16[512,768]{1,0:T(8,128)(2,1)S(1)}, bf16[512,768]{1,0:T(8,128)(2,1)S(1)}, u32[]{:S(2)}, u32[]{:S(2)}) collective-permute-start(bf16[512,768]{1,0:T(8,128)(2,1)S(1)} %rotate_chunk.6), channel_id=1, source_target_pairs={{0,4},{12,8},{1,5},{13,9},{2,6},{14,10},{3,7},{15,11},{16,20},{28,... | collective-permute-start | bytes 2359304 | tf_op jit(solution)/shard_map/ppermute | solution.py:210
  79.6 34.0 %collective-permute-start.3 = (bf16[512,640]{1,0:T(8,128)(2,1)S(1)}, bf16[512,640]{1,0:T(8,128)(2,1)S(1)}, u32[]{:S(2)}, u32[]{:S(2)}) collective-permute-start(bf16[512,640]{1,0:T(8,128)(2,1)S(1)} %pad_maximum_fusion), channel_id=1, source_target_pairs={{0,2},{5,7},{10,8},{15,13},{16,18},{21,23},{26,24},{31,29}} | collective-permute-start | bytes 1966088 | tf_op jit(solution)/shard_map/ppermute | solution.py:184
  86.1 30.5 %collective-permute-start.18 = (bf16[512,512]{1,0:T(8,128)(2,1)S(1)}, bf16[512,512]{1,0:T(8,128)(2,1)S(1)}, u32[]{:S(2)}, u32[]{:S(2)}) collective-permute-start(bf16[512,512]{1,0:T(8,128)(2,1)S(1)} %rotate_chunk.7), channel_id=1, source_target_pairs={{0,4},{12,8},{1,5},{13,9},{2,6},{14,10},{3,7},{15,11},{16,20},{28,... | collective-permute-start | bytes 1572872 | tf_op jit(solution)/shard_map/ppermute | solution.py:210
  92.4 40.2 %collective-permute-start.23 = (bf16[512,768]{1,0:T(8,128)(2,1)S(1)}, bf16[512,768]{1,0:T(8,128)(2,1)S(1)}, u32[]{:S(2)}, u32[]{:S(2)}) collective-permute-start(bf16[512,768]{1,0:T(8,128)(2,1)S(1)} %rotate_chunk.8), channel_id=1, source_target_pairs={{0,4},{12,8},{1,5},{13,9},{2,6},{14,10},{3,7},{15,11},{16,20},{28,... | collective-permute-start | bytes 2359304 | tf_op jit(solution)/shard_map/ppermute | solution.py:210
  93.9 21.3 %collective-permute-start.20 = (bf16[512,512]{1,0:T(8,128)(2,1)S(1)}, bf16[512,512]{1,0:T(8,128)(2,1)S(1)}, u32[]{:S(2)}, u32[]{:S(2)}) collective-permute-start(bf16[512,512]{1,0:T(8,128)(2,1)S(1)} %add_convert_fusion.9), channel_id=1, source_target_pairs={{4,8},{8,4},{5,9},{9,5},{6,10},{10,6},{7,11},{11,7},{20,24},{24,20... | collective-permute-start | bytes 1572872 | tf_op jit(solution)/shard_map/ppermute | solution.py:215
  104.7 21.9 %collective-permute-start.24 = (bf16[512,768]{1,0:T(8,128)(2,1)S(1)}, bf16[512,768]{1,0:T(8,128)(2,1)S(1)}, u32[]{:S(2)}, u32[]{:S(2)}) collective-permute-start(bf16[512,768]{1,0:T(8,128)(2,1)S(1)} %add_convert_fusion.3), channel_id=1, source_target_pairs={{4,8},{8,4},{5,9},{9,5},{6,10},{10,6},{7,11},{11,7},{20,24},{24,20... | collective-permute-start | bytes 2359304 | tf_op jit(solution)/shard_map/ppermute | solution.py:215
  113.6 32.8 %collective-permute-start.17 = (bf16[512,640]{1,0:T(8,128)(2,1)S(1)}, bf16[512,640]{1,0:T(8,128)(2,1)S(1)}, u32[]{:S(2)}, u32[]{:S(2)}) collective-permute-start(bf16[512,640]{1,0:T(8,128)(2,1)S(1)} %rotate_chunk.9), channel_id=1, source_target_pairs={{0,4},{12,8},{1,5},{13,9},{2,6},{14,10},{3,7},{15,11},{16,20},{28,... | collective-permute-start | bytes 1966088 | tf_op jit(solution)/shard_map/ppermute | solution.py:210
  115.1 34.0 %collective-permute-start.4 = (bf16[512,640]{1,0:T(8,128)(2,1)S(1)}, bf16[512,640]{1,0:T(8,128)(2,1)S(1)}, u32[]{:S(2)}, u32[]{:S(2)}) collective-permute-start(bf16[512,640]{1,0:T(8,128)(2,1)S(1)} %broadcast_select_fusion.3), channel_id=1, source_target_pairs={{0,1},{5,4},{10,11},{15,14},{2,3},{7,6},{8,9},{13,12},{16,17},{21,... | collective-permute-start | bytes 1966088 | tf_op jit(solution)/shard_map/ppermute | solution.py:186
  116.6 37.0 %collective-permute-start.31 = (bf16[512,512]{1,0:T(8,128)(2,1)S(1)}, bf16[512,512]{1,0:T(8,128)(2,1)S(1)}, u32[]{:S(2)}, u32[]{:S(2)}) collective-permute-start(bf16[512,512]{1,0:T(8,128)(2,1)S(1)} %add_convert_fusion.8), channel_id=1, source_target_pairs={{4,0},{8,12},{5,1},{9,13},{6,2},{10,14},{7,3},{11,15},{20,16},{24,... | collective-permute-start | bytes 1572872 | tf_op jit(solution)/shard_map/ppermute | solution.py:218
  126.6 15.4 %collective-permute-start.22 = (bf16[512,512]{1,0:T(8,128)(2,1)S(1)}, bf16[512,512]{1,0:T(8,128)(2,1)S(1)}, u32[]{:S(2)}, u32[]{:S(2)}) collective-permute-start(bf16[512,512]{1,0:T(8,128)(2,1)S(1)} %add_convert_fusion.7), channel_id=1, source_target_pairs={{4,8},{8,4},{5,9},{9,5},{6,10},{10,6},{7,11},{11,7},{20,24},{24,20... | collective-permute-start | bytes 1572872 | tf_op jit(solution)/shard_map/ppermute | solution.py:215
  132.8 41.6 %collective-permute-start.27 = (bf16[512,768]{1,0:T(8,128)(2,1)S(1)}, bf16[512,768]{1,0:T(8,128)(2,1)S(1)}, u32[]{:S(2)}, u32[]{:S(2)}) collective-permute-start(bf16[512,768]{1,0:T(8,128)(2,1)S(1)} %add_convert_fusion.1), channel_id=1, source_target_pairs={{4,8},{8,4},{5,9},{9,5},{6,10},{10,6},{7,11},{11,7},{20,24},{24,20... | collective-permute-start | bytes 2359304 | tf_op jit(solution)/shard_map/ppermute | solution.py:215
  146.6 26.3 %collective-permute-start.25 = (bf16[512,640]{1,0:T(8,128)(2,1)S(1)}, bf16[512,640]{1,0:T(8,128)(2,1)S(1)}, u32[]{:S(2)}, u32[]{:S(2)}) collective-permute-start(bf16[512,640]{1,0:T(8,128)(2,1)S(1)} %add_convert_fusion.5), channel_id=1, source_target_pairs={{4,8},{8,4},{5,9},{9,5},{6,10},{10,6},{7,11},{11,7},{20,24},{24,20... | collective-permute-start | bytes 1966088 | tf_op jit(solution)/shard_map/ppermute | solution.py:215
  150.9 25.1 %collective-permute-start.30 = (bf16[512,768]{1,0:T(8,128)(2,1)S(1)}, bf16[512,768]{1,0:T(8,128)(2,1)S(1)}, u32[]{:S(2)}, u32[]{:S(2)}) collective-permute-start(bf16[512,768]{1,0:T(8,128)(2,1)S(1)} %add_convert_fusion.2), channel_id=1, source_target_pairs={{4,0},{8,12},{5,1},{9,13},{6,2},{10,14},{7,3},{11,15},{20,16},{24,... | collective-permute-start | bytes 2359304 | tf_op jit(solution)/shard_map/ppermute | solution.py:218
  152.2 28.5 %collective-permute-start.29 = (bf16[512,512]{1,0:T(8,128)(2,1)S(1)}, bf16[512,512]{1,0:T(8,128)(2,1)S(1)}, u32[]{:S(2)}, u32[]{:S(2)}) collective-permute-start(bf16[512,512]{1,0:T(8,128)(2,1)S(1)} %add_convert_fusion.6), channel_id=1, source_target_pairs={{4,0},{8,12},{5,1},{9,13},{6,2},{10,14},{7,3},{11,15},{20,16},{24,... | collective-permute-start | bytes 1572872 | tf_op jit(solution)/shard_map/ppermute | solution.py:218
  173.0 21.8 %collective-permute-start.26 = (bf16[512,640]{1,0:T(8,128)(2,1)S(1)}, bf16[512,640]{1,0:T(8,128)(2,1)S(1)}, u32[]{:S(2)}, u32[]{:S(2)}) collective-permute-start(bf16[512,640]{1,0:T(8,128)(2,1)S(1)} %add_convert_fusion.4), channel_id=1, source_target_pairs={{4,0},{8,12},{5,1},{9,13},{6,2},{10,14},{7,3},{11,15},{20,16},{24,... | collective-permute-start | bytes 1966088 | tf_op jit(solution)/shard_map/ppermute | solution.py:218
  174.6 36.9 %collective-permute-start.28 = (bf16[512,768]{1,0:T(8,128)(2,1)S(1)}, bf16[512,768]{1,0:T(8,128)(2,1)S(1)}, u32[]{:S(2)}, u32[]{:S(2)}) collective-permute-start(bf16[512,768]{1,0:T(8,128)(2,1)S(1)} %add_convert_fusion), channel_id=1, source_target_pairs={{4,0},{8,12},{5,1},{9,13},{6,2},{10,14},{7,3},{11,15},{20,16},{24,... | collective-permute-start | bytes 2359304 | tf_op jit(solution)/shard_map/ppermute | solution.py:218
  217.6 6.1 %copy-start.1 = (bf16[128,5120]{1,0:T(8,128)(2,1)S(1)}, bf16[128,5120]{1,0:T(8,128)(2,1)}, u32[]{:S(2)}) copy-start(bf16[128,5120]{1,0:T(8,128)(2,1)} %param.5) | copy-start | bytes 3932164
